TPU v7x, 32 devices: a whole 2x2x4 slice. The times are simulated.
32 devices in a mesh: dp: 4 (over y, core), seq: 8 (over z, x).
Axes of the slice: x: 2, y: 2, z: 4, core: 2. Of those that a mesh axis runs over, the one named last changes fastest.
Arguments:
- tokens: bfloat16 [2, 8, 1024, 768], P(None, 'dp', 'seq'), may hold values from -6 to 6
- cotangent: bfloat16 [2, 8, 1024, 768], P(None, 'dp', 'seq'), may hold values from -6 to 6
- stretch_size: int32 [2, 8], P(None, 'dp'), may hold values from 128 to 1024, as said below
- w_value: bfloat16 [768, 1536], P(('dp', 'seq')), may hold values from -0.21875 to 0.21875
- w_base: bfloat16 [768, 3200], P(('dp', 'seq')), may hold values from -0.21875 to 0.21875
- w_out: bfloat16 [1536, 768], P(('dp', 'seq')), may hold values from -1.25 to 1.25
- w_up: bfloat16 [768, 1536], P(('dp', 'seq')), may hold values from -0.21875 to 0.21875
- w_down: bfloat16 [1536, 768], P(('dp', 'seq')), may hold values from -0.15625 to 0.15625
- ema_delta: bfloat16 [768, 16], P(('dp', 'seq')), may hold values from -8 to 0.1
- ema_alpha: bfloat16 [768, 16], P(('dp', 'seq')), may hold values from -9 to -1
- ema_beta: bfloat16 [768, 16], P(('dp', 'seq')), may hold values from -4 to 4
- ema_gamma: bfloat16 [768, 16], P(('dp', 'seq')), may hold values from -4 to 4
- ema_omega: bfloat16 [768], P(('dp', 'seq')), may hold values from -4 to 4
- first_gain: bfloat16 [768], P(('dp', 'seq')), may hold values from 0.5 to 1.5
- second_gain: bfloat16 [768], P(('dp', 'seq')), may hold values from 0.5 to 1.5
- query_gain: float32 [128], replicated, may hold values from -8 to 8
- query_bias: float32 [128], replicated, may hold values from -4 to 4
- key_gain: float32 [128], replicated, may hold values from -8 to 8
- relative_bias: float32 [32], replicated, may hold values from -4 to 4
Outputs:
- block_out: bfloat16 [2, 8, 1024, 768], P(None, 'dp', 'seq')
- grad_tokens: float32 [2, 8, 1024, 768], P(None, 'dp', 'seq')
- grad_w_value: float32 [768, 1536], P(('dp', 'seq'))
- grad_w_base: float32 [768, 3200], P(('dp', 'seq'))
- grad_w_out: float32 [1536, 768], P(('dp', 'seq'))
- grad_w_up: float32 [768, 1536], P(('dp', 'seq'))
- grad_w_down: float32 [1536, 768], P(('dp', 'seq'))
- grad_ema_delta: float32 [768, 16], P(('dp', 'seq'))
- grad_ema_alpha: float32 [768, 16], P(('dp', 'seq'))
- grad_ema_beta: float32 [768, 16], P(('dp', 'seq'))
- grad_ema_gamma: float32 [768, 16], P(('dp', 'seq'))
- grad_ema_omega: float32 [768], P(('dp', 'seq'))
- grad_first_gain: float32 [768], P(('dp', 'seq'))
- grad_second_gain: float32 [768], P(('dp', 'seq'))
- grad_query_gain: float32 [128], replicated
- grad_query_bias: float32 [128], replicated
- grad_key_gain: float32 [128], replicated
- grad_relative_bias: float32 [32], replicated
Inputs may be any that keep to these rules, and one draw needn't show every extreme that they name: `stretch_size`: in each micro-batch, exactly one of the 2 sequences of each index of dp has the value 1024; the others have 128.
All inputs are finite; a program needn't handle non-finite values.
Results may differ from a plain program's by a relative error of at most 0.033.
The roundings to bfloat16 on the way count: a program that leaves them out, or rounds other values in their place, can miss the bound.
Values may be sent and summed in bfloat16 or wider, within the bound.
A program may use at most 384 MiB of HBM per device.

v0:
```python
import functools

import jax
import jax.numpy as jnp
import numpy as np
from jax import lax
from jax.experimental import pallas as pl
from jax.experimental.pallas import tpu as pltpu
from jax.sharding import PartitionSpec as P

epsilon = 1e-05
masked_fill = -1e30
MESH = pl.DeviceIdType.MESH
ANY = pl.BlockSpec(memory_space=pl.ANY)
VM = pl.BlockSpec(memory_space=pltpu.VMEM)
SM = pl.BlockSpec(memory_space=pltpu.SMEM)
F32 = jnp.float32
BF16 = jnp.bfloat16
SEG = 8
LANES = 128


def bucket_edges(bucket_count):
    edge_list = [0]
    middle = bucket_count // 2
    for number in range(1, bucket_count):
        edge_list.append(number if number < middle else int(middle * 2 ** ((number - middle) / 2)))
    return edge_list


class Layout:
    def __init__(self, dp, seq, micro, items):
        self.dp, self.S = dp, seq
        self.C = 2
        self.Y = dp // 2
        self.X = min(self.Y, seq)
        self.Z = seq // self.X
        self.items = items
        self.MS = micro * items
        self.Q = 2 * self.MS
        self.Cq = seq // self.Q
        self.G = 2 * self.Cq
        self.BL = seq // self.G

    def here(self):
        d, b = lax.axis_index("dp"), lax.axis_index("seq")
        return d // 2, d % 2, b // self.X, b % self.X, b


class Wire:
    def __init__(self, lay, send, recv):
        self.lay, self.send, self.recv, self.count = lay, send, recv, 0
        self.sent = []

    def to(self, y, c, z, x):
        return (y * 2 + c, z * self.lay.X + x)

    def start(self, src, dst, target):
        number = self.count
        self.count += 1
        copy = pltpu.make_async_remote_copy(
            src_ref=src,
            dst_ref=dst,
            send_sem=self.send.at[number],
            recv_sem=self.recv.at[number],
            device_id=target,
            device_id_type=MESH,
        )
        copy.start()
        self.sent.append(copy)
        return copy

    def finish(self):
        for copy in self.sent:
            copy.wait_send()


def greet(lay):
    y, c, z, x, b = lay.here()
    barrier = pltpu.get_barrier_semaphore()
    plane = 2 * lay.S

    def one(k, carry):
        other = (c * lay.S + b + k) % plane
        pl.semaphore_signal(
            barrier, inc=1, device_id=(y * 2 + other // lay.S, other % lay.S), device_id_type=MESH
        )
        return carry

    lax.fori_loop(1, plane, one, 0)
    for k in range(1, lay.Y):
        pl.semaphore_signal(
            barrier, inc=1, device_id=(((y + k) % lay.Y) * 2 + c, b), device_id_type=MESH
        )
    pl.semaphore_wait(barrier, plane - 1 + lay.Y - 1)


ALPHA = 0.5
AHEAD = 2
LAG = 2
ORDER = 1
LIMIT = 800


def half_columns(columns):
    return max(1, int(columns // LANES * ALPHA + 0.5)) * LANES


def reshard_in(lay, sources, targets, send, recv, local):
    y, c, z, x, b = lay.here()
    g = b // lay.BL
    slot = b % lay.BL
    qm = b // lay.Cq
    gm = (b % lay.Cq) * 2 + c

    def begin(n):
        for source, target in ((sources[n], targets[n]),):
            for ms in range(lay.MS):
                seq_to = (ms * 2 + c) * lay.Cq + g // 2
                mine = jnp.logical_and(seq_to == b, g % 2 == c)
                block = source.at[ms // lay.items, ms % lay.items]

                @pl.when(jnp.logical_not(mine))
                def _():
                    pltpu.make_async_remote_copy(
                        src_ref=block,
                        dst_ref=target.at[slot],
                        send_sem=send.at[n, ms],
                        recv_sem=recv.at[n, slot],
                        device_id=(y * 2 + g % 2, seq_to),
                        device_id_type=MESH,
                    ).start()

                @pl.when(mine)
                def _():
                    pltpu.make_async_copy(block, target.at[slot], local.at[n]).start()

    def wait(n):
        source, target = sources[n], targets[n]
        for ms in range(lay.MS):
            seq_to = (ms * 2 + c) * lay.Cq + g // 2
            mine = jnp.logical_and(seq_to == b, g % 2 == c)
            block = source.at[ms // lay.items, ms % lay.items]

            @pl.when(jnp.logical_not(mine))
            def _():
                pltpu.make_async_remote_copy(
                    src_ref=block,
                    dst_ref=target.at[slot],
                    send_sem=send.at[n, ms],
                    recv_sem=recv.at[n, slot],
                    device_id=(y * 2 + g % 2, seq_to),
                    device_id_type=MESH,
                ).wait_send()

            @pl.when(mine)
            def _():
                pltpu.make_async_copy(block, target.at[slot], local.at[n]).wait()

        for j in range(lay.BL):
            from_b = gm * lay.BL + j
            own = jnp.logical_and(from_b == b, qm % 2 == c)

            @pl.when(jnp.logical_not(own))
            def _():
                pltpu.make_async_remote_copy(
                    src_ref=source.at[0, 0],
                    dst_ref=target.at[j],
                    send_sem=send.at[n, 0],
                    recv_sem=recv.at[n, j],
                    device_id=(y * 2 + qm % 2, from_b),
                    device_id_type=MESH,
                ).wait_recv()

    return begin, wait


def reshard_out(lay, sources, targets, send, recv, local):
    y, c, z, x, b = lay.here()
    g = b // lay.BL
    qm = b // lay.Cq
    gm = (b % lay.Cq) * 2 + c
    ms_to = qm // 2
    m_to, s_to = ms_to // lay.items, ms_to % lay.items

    def copies(n, j):
        from_b = gm * lay.BL + j
        own = jnp.logical_and(from_b == b, qm % 2 == c)
        remote = pltpu.make_async_remote_copy(
            src_ref=sources[n].at[j],
            dst_ref=targets[n].at[m_to, s_to],
            send_sem=send.at[n, j],
            recv_sem=recv.at[n, ms_to],
            device_id=(y * 2 + qm % 2, from_b),
            device_id_type=MESH,
        )
        near = pltpu.make_async_copy(sources[n].at[j], targets[n].at[m_to, s_to], local.at[n])
        return own, remote, near

    def begin(n):
        for j in range(lay.BL):
            own, remote, near = copies(n, j)
            pl.when(jnp.logical_not(own))(remote.start)
            pl.when(own)(near.start)

    def wait(n):
        for j in range(lay.BL):
            own, remote, near = copies(n, j)
            pl.when(jnp.logical_not(own))(remote.wait_send)
            pl.when(own)(near.wait)
        for ms in range(lay.MS):
            seq_at = (ms * 2 + c) * lay.Cq + g // 2
            own = jnp.logical_and(seq_at == b, g % 2 == c)

            @pl.when(jnp.logical_not(own))
            def _():
                pltpu.make_async_remote_copy(
                    src_ref=sources[n].at[0],
                    dst_ref=targets[n].at[ms // lay.items, ms % lay.items],
                    send_sem=send.at[n, 0],
                    recv_sem=recv.at[n, ms],
                    device_id=(y * 2 + g % 2, seq_at),
                    device_id_type=MESH,
                ).wait_recv()

    return begin, wait


def chunks_of(shapes, limit):
    result = []
    for n, shape in enumerate(shapes):
        tiles = shape[-1] // LANES
        cuts = max(1, -(-shape[0] * shape[-1] // limit))
        at = 0
        for cut in range(cuts):
            width = (tiles - at) // (cuts - cut) if cut == cuts - 1 else -(-(tiles - at) // (cuts - cut))
            result.append((n, at * LANES, width * LANES))
            at += width
    return result


def column_blocks(columns, most=768):
    cuts = -(-columns // most)
    while (columns // LANES) % cuts:
        cuts += 1
    width = columns // cuts
    return [(i * width, width) for i in range(cuts)]


def weight_block(full, stage, sem, at, width):
    target = stage.at[:, :, :, :, :, pl.ds(0, width)]
    copy = pltpu.make_async_copy(full.at[:, :, :, :, :, pl.ds(at, width)], target, sem)
    copy.start()
    copy.wait()
    block = stage[:, :, :, :, :, 0:width]
    return block.reshape(-1, width)


def gather_kernel(lay, count, chunks, refs):
    tok, cot = refs[0], refs[1]
    shards = refs[2 : 2 + count]
    tok_out, cot_out = refs[2 + count], refs[3 + count]
    fulls = refs[4 + count : 4 + 2 * count]
    send, recv, local, t_send, t_recv, t_local = refs[4 + 2 * count :]
    y, c, z, x, b = lay.here()
    X, Y, Z = lay.X, lay.Y, lay.Z
    greet(lay)
    wire = Wire(lay, send, recv)
    begin, wait = reshard_in(lay, (tok, cot), (tok_out, cot_out), t_send, t_recv, t_local)
    total = len(chunks)
    owns = []
    for i, (n, at, width) in enumerate(chunks):
        cols = pl.ds(at, width)
        copy = pltpu.make_async_copy(
            shards[n].at[:, cols], fulls[n].at[y, c, z, x, :, cols], local.at[i]
        )
        copy.start()
        owns.append(copy)
    arrived = [dict() for i in range(total)]

    def stage_z(i):
        n, at, width = chunks[i]
        cols = pl.ds(at, width)
        arrived[i]["z"] = [
            wire.start(
                shards[n].at[:, cols],
                fulls[n].at[y, c, z, x, :, cols],
                wire.to(y, c, (z + k) % Z, x),
            )
            for k in range(1, Z)
        ]

    def parts(i):
        n, at, width = chunks[i]
        left = half_columns(width)
        result = [(at, left)]
        if left < width:
            result.append((at + left, width - left))
        return result

    def to_core(i, block):
        arrived[i].setdefault("core", []).append(wire.start(block, block, wire.to(y, 1 - c, z, x)))

    def stage_one(i):
        owns[i].wait()
        for copy in arrived[i]["z"]:
            copy.wait_recv()
        n, first, columns = chunks[i]
        full = fulls[n]
        for half, (at, width) in enumerate(parts(i)):
            block = full.at[y, c, :, x, :, pl.ds(at, width)]
            if half == 0:
                arrived[i]["x0"] = [
                    wire.start(block, block, wire.to(y, c, z, (x + k) % X)) for k in range(1, X)
                ]
            else:
                arrived[i]["y1"] = [
                    wire.start(block, block, wire.to((y + k) % Y, c, z, x)) for k in range(1, Y)
                ]
        to_core(i, full.at[y, c, :, x, :, pl.ds(first, columns)])

    def stage_two(i):
        full = fulls[chunks[i][0]]
        for half, (at, width) in enumerate(parts(i)):
            cols = pl.ds(at, width)
            if half == 0:
                for copy in arrived[i]["x0"]:
                    copy.wait_recv()
                block = full.at[y, c, :, :, :, cols]
                arrived[i]["y0"] = [
                    wire.start(block, block, wire.to((y + k) % Y, c, z, x)) for k in range(1, Y)
                ]
                for k in range(1, X):
                    to_core(i, full.at[y, c, :, (x + X - k) % X, :, cols])
            else:
                for copy in arrived[i]["y1"]:
                    copy.wait_recv()
                block = full.at[:, c, :, x, :, cols]
                arrived[i]["x1"] = [
                    wire.start(block, block, wire.to(y, c, z, (x + k) % X)) for k in range(1, X)
                ]
                for k in range(1, Y):
                    to_core(i, full.at[(y + Y - k) % Y, c, :, x, :, cols])

    def stage_three(i):
        full = fulls[chunks[i][0]]
        for half, (at, width) in enumerate(parts(i)):
            cols = pl.ds(at, width)
            if half == 0:
                for k, copy in enumerate(arrived[i]["y0"], 1):
                    copy.wait_recv()
                    to_core(i, full.at[(y + Y - k) % Y, c, :, :, :, cols])
            else:
                for k, copy in enumerate(arrived[i]["x1"], 1):
                    copy.wait_recv()
                    to_core(i, full.at[:, c, :, (x + X - k) % X, :, cols])

    def finish():
        for i in range(total):
            for copy in arrived[i]["core"]:
                copy.wait_recv()
        wire.finish()

    def gathered(n):
        for i in range(total):
            if chunks[i][0] == n:
                for copy in arrived[i].pop("core"):
                    copy.wait_recv()
                arrived[i]["core"] = []

    return wire, (begin, wait), (stage_z, stage_one, stage_two, stage_three), gathered, finish


def group_copies(lay, send, recv, source, inbox, forward):
    y, c, z, x, b = lay.here()
    q = b // lay.Cq
    g = (b % lay.Cq) * 2 + c
    copies = []
    for k in range(1, lay.G):
        t = (g + (k if forward else lay.G - k)) % lay.G
        copies.append(
            pltpu.make_async_remote_copy(
                src_ref=source,
                dst_ref=inbox.at[k - 1],
                send_sem=send.at[k - 1],
                recv_sem=recv.at[k - 1],
                device_id=(y * 2 + t % 2, q * lay.Cq + t // 2),
                device_id_type=MESH,
            )
        )
    return copies, g


def to_tiles(low, tiles, r0, rows):
    for t in range(tiles.shape[0]):
        tiles[t, pl.ds(r0, rows), :] = low[:, t * LANES : (t + 1) * LANES].astype(F32)


def make_tables(lay, H, pack, raw, table, turned):
    r = pack.shape[4]
    total = lay.Y * 2 * lay.Z * lay.X

    def one(i, carry):
        block = pack[i // (2 * lay.Z * lay.X), i // (lay.Z * lay.X) % 2, i // lay.X % lay.Z, i % lay.X]
        raw[pl.ds(i * r, r), :] = block.astype(F32)
        return carry

    lax.fori_loop(0, total, one, 0)
    for t in range(table.shape[0]):
        v = raw[t * LANES : (t + 1) * LANES, :].T
        turned[t] = v
        leak = jax.nn.sigmoid(v[:H])
        decay = 1.0 - leak * jax.nn.sigmoid(v[H : 2 * H])
        table[t, :H] = decay
        table[t, H : 2 * H] = jnp.log(decay)
        table[t, 2 * H : 3 * H] = leak * v[2 * H : 3 * H] * v[3 * H : 4 * H] * (H ** (-0.5))


def carry_in(lay, H, rows, g, inbox, table, inc, t, later):
    log = table[t, H : 2 * H]
    state = jnp.zeros((H, LANES), F32)
    slope = jnp.zeros((H, LANES), F32)
    for k in range(1, lay.G):
        span = (k - 1) * rows
        valid = (g + k < lay.G) if later else (k <= g)
        s_part = inbox[k - 1, t, :H]
        r_part = s_part * 0.0 if later else inbox[k - 1, t, H : 2 * H]
        if span:
            power = jnp.exp(span * log)
            r_part = power * r_part + (span * jnp.exp((span - 1) * log)) * s_part
            s_part = power * s_part
        state = state + jnp.where(valid, s_part, 0.0)
        slope = slope + jnp.where(valid, r_part, 0.0)
    inc[t, :H] = state
    if not later:
        inc[t, H : 2 * H] = slope


def forward_kernel(lay, count, chunks, H, refs):
    n_in, n_out = 2 + count, 15 + count
    ins = refs[:n_in]
    query_gain, query_bias, key_gain, relative = refs[n_in : n_in + 4]
    refs = refs[n_in + 4 :]
    outs, scratch = refs[:n_out], refs[n_out:]
    tok_out, cot_out = outs[0], outs[1]
    fulls = outs[2 : 2 + count]
    mixed, ema, si, ri, table, turned = outs[2 + count : 8 + count]
    value_pre, base, queries, keys, vals, probs, attended = outs[8 + count :]
    sems, work = scratch[:6], scratch[6:]
    xt, pack, raw, s_end, r_end, mine, inbox, inc, stage, strip, scores, load, c_send, c_recv = work
    wire, (begin, wait), stages, gathered, finish = gather_kernel(
        lay, count, chunks, ins + (tok_out, cot_out) + tuple(fulls) + sems
    )
    stage_z, stage_one, stage_two, stage_three = stages
    total = len(chunks)
    rows = xt.shape[1]
    tiles = xt.shape[0]
    copies, g = group_copies(lay, c_send.at[0], c_recv.at[0], mine, inbox, True)
    others = pl.ds(1, lay.G - 1)
    vals_copies, g = group_copies(
        lay, c_send.at[1], c_recv.at[1], vals.at[0], vals.at[others], True
    )
    keys_copies, g = group_copies(
        lay, c_send.at[2], c_recv.at[2], keys.at[0], keys.at[others], True
    )
    width = tok_out.shape[2]
    zw = queries.shape[1]

    def value(at, cols):
        v = mm(tok_out[...].reshape(rows, width), weight_block(fulls[1], stage, load, at, cols))
        value_pre[:, at : at + cols] = v
        vals[0, :, at : at + cols] = (v * jax.nn.sigmoid(v)).astype(BF16)

    def send_values():
        for copy in vals_copies:
            copy.start()

    def bias():
        bias_kernel(lay.G * rows, relative.shape[0], relative, strip)

    def base_out(at, cols):
        base[:, at : at + cols] = mm(mixed[...], weight_block(fulls[2], stage, load, at, cols))

    def send_keys():
        z_pre = base[:, :zw]
        shared = z_pre * jax.nn.sigmoid(z_pre)
        queries[...] = (shared * query_gain[...] + query_bias[...]).astype(BF16)
        keys[0] = (shared * key_gain[...]).astype(BF16)
        for copy in keys_copies:
            copy.start()

    def keys_here():
        for copy in keys_copies + vals_copies:
            copy.wait()

    def attend(part):
        y, c, z, x, b = lay.here()
        q_at = b // lay.Cq
        first = ((y * 2 + q_at % 2) * lay.Z * lay.X) * pack.shape[4]
        marks = raw[pl.ds(first, 1), :]
        lane = lax.broadcasted_iota(jnp.int32, (1, LANES), 1)
        mark = jnp.sum(
            jnp.where(lane == 4 * H + 3 + q_at // 2, marks, 0.0), axis=1, keepdims=True
        )
        far = jnp.where(mark == float(lay.G * rows), 0.0, masked_fill)
        attend_body(lay, g, far, queries, strip, keys, vals, attended, probs, scores, part)

    def tables():
        gathered(0)
        copy = pltpu.make_async_copy(fulls[0], pack, load)
        copy.start()
        copy.wait()
        make_tables(lay, H, pack, raw, table, turned)

    def tokens():
        wait(0)
        for j in range(lay.BL):
            to_tiles(tok_out[j], xt, j * (rows // lay.BL), rows // lay.BL)

    def ends(first, last):
        def one(t, carry):
            ema_ends_kernel(H, xt.at[t], table.at[t], s_end.at[t], r_end.at[t])
            for h in range(H):
                mine[t, pl.ds(h, 1), :] = s_end[t, h, SEG - 1 : SEG, :]
                mine[t, pl.ds(H + h, 1), :] = r_end[t, h, SEG - 1 : SEG, :]
            return carry

        lax.fori_loop(first, last, one, 0)

    def exchange():
        for copy in copies:
            copy.start()

    def carries():
        for copy in copies:
            copy.wait()
        for t in range(tiles):
            carry_in(lay, H, rows, g, inbox, table, inc, t, False)

    def out(first, last):
        def one(t, carry):
            ema_out_kernel(
                H, xt.at[t], table.at[t], turned.at[t, pl.ds(4 * H, 1)], s_end.at[t], r_end.at[t],
                inc.at[t], ema.at[t], si.at[t], ri.at[t],
            )
            return carry

        lax.fori_loop(first, last, one, 0)
        for t in range(first, last):
            for r0 in range(0, rows, 128):
                v = ema[t, pl.ds(r0, 128), :]
                mixed[pl.ds(r0, 128), t * LANES : (t + 1) * LANES] = (
                    v * jax.nn.sigmoid(v)
                ).astype(BF16)

    steps = [lambda: begin(0)]
    last = {}
    for i in range(min(AHEAD, total)):
        steps.append(functools.partial(stage_z, i))
    for turn in range(total + 2 * LAG):
        if 0 <= turn - 2 * LAG < total:
            last[chunks[turn - 2 * LAG][0]] = len(steps)
            steps.append(functools.partial(stage_three, turn - 2 * LAG))
        if 0 <= turn - LAG < total:
            steps.append(functools.partial(stage_two, turn - LAG))
        if turn < total:
            steps.append(functools.partial(stage_one, turn))
        if turn + AHEAD < total:
            steps.append(functools.partial(stage_z, turn + AHEAD))
        if turn == PLAN[5]:
            steps.append(lambda: begin(1))
    base_blocks = column_blocks(base.shape[1])
    todo = [(last[0] + PLAN[0], tables), (PLAN[1], tokens)]
    todo += [(0, functools.partial(ends, t, t + 1)) for t in range(tiles)]
    todo += [(0, exchange)]
    todo += [(last[1] + PLAN[2], lambda: gathered(1))]
    todo += [(0, functools.partial(value, *block)) for block in column_blocks(vals.shape[2])]
    todo += [(0, send_values), (0, carries)]
    todo += [(0, functools.partial(out, t, t + 1)) for t in range(tiles)]
    todo += [(0, bias), (last[2] + PLAN[3], lambda: gathered(2))]
    todo += [(0, functools.partial(base_out, *base_blocks[0])), (0, send_keys)]
    todo += [(0, functools.partial(base_out, *block)) for block in base_blocks[1:]]
    todo += [(0, keys_here)]
    todo += [(0, functools.partial(attend, part)) for part in range(rows // QB)]
    interleave(steps, todo, PLAN[6])
    finish()
    wait(1)


def interleave(steps, todo, most):
    todo = list(todo)
    done = set()

    def run():
        first, piece, name = (todo.pop(0) + (None,))[:3]
        piece()
        done.add(name)

    for number, step in enumerate(steps):
        step, needs = step if isinstance(step, tuple) else (step, None)
        while needs is not None and needs not in done:
            run()
        step()
        for i in range(most):
            if todo and todo[0][0] <= number:
                run()
    while todo:
        run()


PLAN = (1, 12, 1, 1, 0, 9, 1)


def forward_all(lay, H, tokens, cotangent, shards, query_gain, query_bias, key_gain, relative):
    count = len(shards)
    chunks = chunks_of([shard.shape for shard in shards], shards[0].shape[0] * LIMIT)
    micro, items, rows, width = tokens.shape
    per = (lay.Z - 1) + 2 * (lay.X - 1 + lay.Y - 1) + 1 + 2 * (lay.X - 1 + lay.Y - 1)
    blocks = jax.ShapeDtypeStruct((lay.BL, rows, width), BF16)
    fulls = [
        jax.ShapeDtypeStruct((lay.Y, 2, lay.Z, lay.X) + shard.shape, shard.dtype)
        for shard in shards
    ]
    T, R = width // LANES, lay.BL * rows
    state = (T, H, SEG, LANES)
    outs = [blocks, blocks] + fulls
    outs += [
        jax.ShapeDtypeStruct((R, width), BF16),
        jax.ShapeDtypeStruct((T, R, LANES), F32),
        jax.ShapeDtypeStruct(state, F32),
        jax.ShapeDtypeStruct(state, F32),
        jax.ShapeDtypeStruct((T, 3 * H, LANES), F32),
        jax.ShapeDtypeStruct((T, LANES, LANES), F32),
    ]
    V, cols, zw, G = shards[1].shape[1], shards[2].shape[1], query_gain.shape[1], lay.G
    outs += [
        jax.ShapeDtypeStruct((R, V), F32),
        jax.ShapeDtypeStruct((R, cols), F32),
        jax.ShapeDtypeStruct((R, zw), BF16),
        jax.ShapeDtypeStruct((G, R, zw), BF16),
        jax.ShapeDtypeStruct((G, R, V), BF16),
        jax.ShapeDtypeStruct((G, R, R), BF16),
        jax.ShapeDtypeStruct((R, V), F32),
    ]

    def body(*refs):
        forward_kernel(lay, count, chunks, H, refs)

    result = pl.pallas_call(
        body,
        out_shape=outs,
        in_specs=[ANY] * (2 + count) + [VM] * 3 + [SM],
        out_specs=[VM] + [ANY] * (1 + count) + [VM] * 13,
        scratch_shapes=[
            pltpu.SemaphoreType.DMA((len(chunks) * per,)),
            pltpu.SemaphoreType.DMA((len(chunks) * per,)),
            pltpu.SemaphoreType.DMA((len(chunks),)),
            pltpu.SemaphoreType.DMA((2, lay.MS)),
            pltpu.SemaphoreType.DMA((2, lay.BL)),
            pltpu.SemaphoreType.DMA((2,)),
            pltpu.VMEM((T, R, LANES), F32),
            pltpu.VMEM(fulls[0].shape, fulls[0].dtype),
            pltpu.VMEM((width, LANES), F32),
            pltpu.VMEM(state, F32),
            pltpu.VMEM(state, F32),
            pltpu.VMEM((T, 2 * H, LANES), F32),
            pltpu.VMEM((lay.G - 1, T, 2 * H, LANES), F32),
            pltpu.VMEM((T, 2 * H, LANES), F32),
            pltpu.VMEM((lay.Y, 2, lay.Z, lay.X, shards[1].shape[0], 768), BF16),
            pltpu.VMEM((QB, (G + 1) * R), F32),
            pltpu.VMEM((QB, G * R), F32),
            pltpu.SemaphoreType.DMA,
            pltpu.SemaphoreType.DMA((3, lay.G - 1)),
            pltpu.SemaphoreType.DMA((3, lay.G - 1)),
        ],
        compiler_params=pltpu.CompilerParams(
            collective_id=0, has_side_effects=True, vmem_limit_bytes=58 * 2**20
        ),
        name="forward_all",
    )(tokens, cotangent, *shards, query_gain, query_bias, key_gain, relative)
    return result[0], result[1], result[2 : 2 + count], result[2 + count :]


def add_blocks(total, index, extra, extra_index, counts, width_at):
    size = int(np.prod(counts)) if counts else 1

    def one(i, carry):
        places = []
        for extent in reversed(counts):
            places.insert(0, i % extent)
            i = i // extent
        a, e = index(*places), extra_index(*places)
        summed = total[a].astype(F32) + extra[e].astype(F32)
        total[a] = summed.astype(total.dtype)
        return carry

    lax.fori_loop(0, size, one, 0)


def scatter_kernel(lay, H, NB, chunks, ins, outs, scratch):
    (
        grads, x_low, d_in, d_att, delta, queries, keys, vals, probs, z_pre, gains_small, mixed, ema,
        base_rest, value_pre, w_base, w_value, pre, gains, table, turned, si, ri, block_out,
    ) = ins
    results, small_out, outs_to, made, dvo, dvi = outs
    bufs, own = scratch[: 6 * len(chunks)], scratch[6 * len(chunks) :]
    small_acc, small_recv, send, recv, local, t_send, t_recv, t_local = own[:8]
    xt, dt, dx, sums, flat, split, l_end, mine, inbox, inc, gx, c_send, c_recv = own[8:21]
    stage, vstage, bstage, pstage, ds, strip, dq, dko, dki, zlow, vlow, mixed_acc, x_acc, load = own[21:35]
    halves = own[35:]
    grads = grads + made + (split,)
    y, c, z, x, b = lay.here()
    X, Y, Z = lay.X, lay.Y, lay.Z
    greet(lay)
    wire = Wire(lay, send, recv)
    begin, wait = reshard_out(lay, (block_out, gx), outs_to, t_send, t_recv, t_local)
    total = len(chunks)
    arrived = [dict() for i in range(total)]

    def buf(i, name):
        return bufs[6 * i + ("acc", "x0", "y1", "y0", "x1", "z").index(name)]

    def parts(i):
        n, at, width = chunks[i]
        left = half_columns(width)
        result = [(0, left)]
        if left < width:
            result.append((left, width - left))
        return result

    def own_half(i):
        n, at, width = chunks[i]
        if n == len(grads) - 1:
            return None
        source = grads[n].at[:, c, :, :, :, pl.ds(at, width)]
        return pltpu.make_async_copy(source, half_of(i), local.at[i])

    def half_of(i):
        n, at, width = chunks[i]
        r = grads[n].shape[4]
        room = [h for h in halves if h.shape[4] == r][0]
        return room.at[i % 2, :, :, :, :, pl.ds(0, width)]

    def stage_core(i):
        n, at, width = chunks[i]
        arrived[i]["core"] = wire.start(
            grads[n].at[:, 1 - c, :, :, :, pl.ds(at, width)],
            buf(i, "acc"),
            wire.to(y, 1 - c, z, x),
        )

    def stage_one(i):
        n, first, columns = chunks[i]
        acc = buf(i, "acc")
        near = own_half(i)
        if near is not None:
            near.start()
            near.wait()
        arrived[i]["core"].wait_recv()
        if near is not None:
            mine_half = half_of(i)
            add_blocks(acc, lambda *p: p, mine_half, lambda *p: p, (Y, Z, X), None)
        else:
            add_blocks(
                acc, lambda *p: p, split, lambda p, q, s: (p, c, q, s), (Y, Z, X), None
            )
        for half, (at, width) in enumerate(parts(i)):
            cols = pl.ds(at, width)
            if half == 0:
                arrived[i]["x0"] = [
                    wire.start(
                        acc.at[:, :, (x + k) % X, :, cols],
                        buf(i, "x0").at[k - 1],
                        wire.to(y, c, z, (x + k) % X),
                    )
                    for k in range(1, X)
                ]
            else:
                arrived[i]["y1"] = [
                    wire.start(
                        acc.at[(y + k) % Y, :, :, :, cols],
                        buf(i, "y1").at[k - 1],
                        wire.to((y + k) % Y, c, z, x),
                    )
                    for k in range(1, Y)
                ]

    def stage_two(i):
        acc = buf(i, "acc")
        for half, (at, width) in enumerate(parts(i)):
            cols = slice(at, at + width)
            view = pl.ds(at, width)
            if half == 0:
                for k, copy in enumerate(arrived[i]["x0"]):
                    copy.wait_recv()
                    add_blocks(
                        acc,
                        lambda p, q: (p, q, x, slice(None), cols),
                        buf(i, "x0"),
                        lambda p, q: (k, p, q),
                        (Y, Z),
                        None,
                    )
                arrived[i]["y0"] = [
                    wire.start(
                        acc.at[(y + k) % Y, :, x, :, view],
                        buf(i, "y0").at[k - 1],
                        wire.to((y + k) % Y, c, z, x),
                    )
                    for k in range(1, Y)
                ]
            else:
                for k, copy in enumerate(arrived[i]["y1"]):
                    copy.wait_recv()
                    add_blocks(
                        acc,
                        lambda p, q: (y, p, q, slice(None), cols),
                        buf(i, "y1"),
                        lambda p, q: (k, p, q),
                        (Z, X),
                        None,
                    )
                arrived[i]["x1"] = [
                    wire.start(
                        acc.at[y, :, (x + k) % X, :, view],
                        buf(i, "x1").at[k - 1],
                        wire.to(y, c, z, (x + k) % X),
                    )
                    for k in range(1, X)
                ]

    def stage_three(i):
        acc = buf(i, "acc")
        for half, (at, width) in enumerate(parts(i)):
            cols = slice(at, at + width)
            name = "y0" if half == 0 else "x1"
            for k, copy in enumerate(arrived[i][name]):
                copy.wait_recv()
                add_blocks(
                    acc,
                    lambda p: (y, p, x, slice(None), cols),
                    buf(i, name),
                    lambda p: (k, p),
                    (Z,),
                    None,
                )
        arrived[i]["z"] = [
            wire.start(
                acc.at[y, (z + k) % Z, x], buf(i, "z").at[k - 1], wire.to(y, c, (z + k) % Z, x)
            )
            for k in range(1, Z)
        ]

    def stage_four(i):
        n, at, width = chunks[i]
        total = buf(i, "acc")[y, z, x].astype(F32)
        for k, copy in enumerate(arrived[i]["z"]):
            copy.wait_recv()
            total = total + buf(i, "z")[k].astype(F32)
        results[n][:, pl.ds(at, width)] = total

    small_at = [0]

    def small_stage(moves):
        copies = []
        for target in moves:
            slot = small_at[0]
            small_at[0] += 1
            copies.append((slot, wire.start(small_acc, small_recv.at[slot], target)))
        for slot, copy in copies:
            copy.wait_send()
            wire.sent = [other for other in wire.sent if other is not copy]
        for slot, copy in copies:
            copy.wait_recv()
            small_acc[...] += small_recv[slot]

    rows, tiles = xt.shape[1], xt.shape[0]
    per_block = rows // lay.BL
    copies, g = group_copies(lay, c_send.at[0], c_recv.at[0], mine, inbox, False)
    G, zw = lay.G, queries.shape[1]
    D = x_low.shape[2]
    scale = zw ** (-0.5)
    n_base, n_value = len(grads) - 3, len(grads) - 2
    q_at = b // lay.Cq

    def back_copy(k, source, target, kind):
        t = (g + G - k) % G
        return pltpu.make_async_remote_copy(
            src_ref=source,
            dst_ref=target,
            send_sem=c_send.at[kind, k - 1],
            recv_sem=c_recv.at[kind, k - 1],
            device_id=(y * 2 + t % 2, q_at * lay.Cq + t // 2),
            device_id_type=MESH,
        )

    key_copies = [back_copy(k, dko.at[k - 1], dki.at[k - 1], 1) for k in range(1, G)]
    val_copies = [back_copy(k, dvo.at[k - 1], dvi.at[k - 1], 2) for k in range(1, G)]

    def fetch(source, target):
        copy = pltpu.make_async_copy(source, target, load)
        copy.start()
        copy.wait()

    def keep_grad(n, at, grad):
        columns = grad.shape[1]
        r = made[n].shape[4]
        low = grad.astype(BF16).reshape(Y, 2, Z, X, r, columns)
        stage[:, :, :, :, :, :columns] = low
        fetch(stage.at[:, :, :, :, :, pl.ds(0, columns)], made[n].at[:, :, :, :, :, pl.ds(at, columns)])

    def base_block(at, columns, first):
        block = bstage.at[:, pl.ds(0, columns)]
        if at == 0:
            bstage[:, :zw] = zlow[...]
            fetch(base_rest.at[:, pl.ds(0, columns - zw)], bstage.at[:, pl.ds(zw, columns - zw)])
        else:
            fetch(base_rest.at[:, pl.ds(at - zw, columns)], block)
        low = block[...]
        keep_grad(0, at, dot_t(mixed[...], low))
        part = mm_t(low, weight_block(w_base, stage, load, at, columns))
        mixed_acc[...] = part if first else mixed_acc[...] + part

    def load_values(k):
        fetch(vals.at[k], vstage)
        if k == G - 1:
            strip[...] = jnp.zeros(strip.shape, F32)

    def scores_back(k, i):
        at = i * QB
        here = pl.ds(at, QB)
        owner = lax.rem(g - k + G, G)
        dw = mm_t(d_att[here, :], vstage[...])
        p = probs[k, here, :].astype(F32)
        grad = p * (dw - delta[here, :])
        off = jnp.clip(G * rows - rows * (g - owner) - at, 0, G * rows)
        strip[:, pl.ds(pl.multiple_of(off, LANES), rows)] += grad
        low = grad.astype(BF16)
        ds[here, :] = low
        part = mm(low, keys[k]) * scale
        dq[here, :] = part if k == G - 1 else dq[here, :] + part

    def keys_back(k):
        grad = dot_t(ds[...], queries[...]) * scale
        if k:
            dko[k - 1] = grad.astype(BF16)
            key_copies[k - 1].start()
        else:
            for copy in key_copies:
                copy.wait()
            for j in range(1, G):
                grad = grad + dki[j - 1].astype(F32)
            pre_z = z_pre[...]
            gate = jax.nn.sigmoid(pre_z)
            shared = pre_z * gate
            small_acc[0:1, :] = jnp.sum(dq[...] * shared, axis=0, keepdims=True)
            small_acc[1:2, :] = jnp.sum(dq[...], axis=0, keepdims=True)
            small_acc[2:3, :] = jnp.sum(grad * shared, axis=0, keepdims=True)
            d_shared = dq[...] * gains_small[0:1, :] + grad * gains_small[1:2, :]
            zlow[...] = (d_shared * (gate * (1.0 + pre_z * (1.0 - gate)))).astype(BF16)

    def values_back(k):
        for at, columns in column_blocks(vstage.shape[1]):
            vstage[:, at : at + columns] = dot_t(
                probs[k], d_att[:, at : at + columns]
            ).astype(BF16)
        fetch(vstage, dvo.at[k - 1])
        val_copies[k - 1].start()

    def buckets():
        sums_of = bucket_sums(G * rows, NB, strip)
        lane = lax.broadcasted_iota(jnp.int32, (1, LANES), 1)
        line = jnp.zeros((1, LANES), F32)
        for k in range(NB):
            line = jnp.where(lane == k, jnp.sum(sums_of[k], axis=1, keepdims=True), line)
        small_acc[3:4, :] = line
        small_acc[4:8, :] = jnp.zeros((4, LANES), F32)

    def values_here():
        for copy in val_copies:
            copy.wait()

    def value_block(at, columns, first):
        cols = pl.ds(at, columns)
        grad = dot_t(probs[0], d_att[:, at : at + columns])
        for k in range(1, G):
            fetch(dvi.at[k - 1, :, cols], bstage.at[:, pl.ds(0, columns)])
            grad = grad + bstage[:, :columns].astype(F32)
        fetch(value_pre.at[:, cols], pstage.at[:, pl.ds(0, columns)])
        v = pstage[:, :columns]
        gate = jax.nn.sigmoid(v)
        vlow[:, :columns] = (grad * (gate * (1.0 + v * (1.0 - gate)))).astype(BF16)
        keep_grad(1, at, dot_t(x_low[...].reshape(rows, D), vlow[:, :columns]))
        part = mm_t(vlow[:, :columns], weight_block(w_value, stage, load, at, columns))
        if first:
            fetch(pre, x_acc)
        x_acc[...] += part

    def d_ema(t):
        v = ema[t]
        gate = jax.nn.sigmoid(v)
        dt[t] = mixed_acc[:, t * LANES : (t + 1) * LANES] * (gate * (1.0 + v * (1.0 - gate)))

    def tile_x():
        for j in range(lay.BL):
            to_tiles(x_low[j], xt, j * per_block, per_block)

    def ends(t):
        ema_back_ends_kernel(H, dt.at[t], table.at[t], l_end.at[t])
        for h in range(H):
            mine[t, pl.ds(h, 1), :] = l_end[t, h, 0:1, :]

    def exchange():
        for copy in copies:
            copy.start()

    def carries():
        for copy in copies:
            copy.wait()
        for t in range(tiles):
            carry_in(lay, H, rows, g, inbox, table, inc, t, True)

    def correlate(t):
        ema_sums_kernel(H, xt.at[t], dt.at[t], table.at[t], si.at[t], ri.at[t], sums.at[t])

    def back(t):
        ema_back_kernel(
            H, dt.at[t], table.at[t], turned.at[t, pl.ds(4 * H, 1)], l_end.at[t], inc.at[t], dx.at[t]
        )
        cols = slice(t * LANES, (t + 1) * LANES)
        for j in range(lay.BL):
            at = pl.ds(j * per_block, per_block)
            gx[j, :, cols] = (x_acc[at, cols] + dx[t, at, :]).astype(BF16)

    def share_sums():
        r = split.shape[4]
        for t in range(tiles):
            sums[t, pl.ds(2 * H + 1, 2), :] = gains[0:2, t * LANES : (t + 1) * LANES]
            flat[t * LANES : (t + 1) * LANES, :] = sums[t].T

        def one(i, carry):
            split[i // (2 * Z * X), i // (Z * X) % 2, i // X % Z, i % X] = flat[pl.ds(i * r, r), :]
            return carry

        lax.fori_loop(0, 2 * X * Y * Z, one, 0)

    sums[...] = jnp.zeros(sums.shape, F32)
    xs = [wire.to(y, c, z, (x + k) % X) for k in range(1, X)]
    ys = [wire.to((y + k) % Y, c, z, x) for k in range(1, Y)]
    zs = [wire.to(y, c, (z + k) % Z, x) for k in range(1, Z)]

    run = functools.partial
    base_blocks = column_blocks(w_base.shape[5])
    value_blocks = column_blocks(w_value.shape[5])
    todo = []
    for number, block in enumerate(base_blocks[1:]):
        todo.append((0, run(base_block, *block, number == 0), (n_base, block[0])))
    for k in list(range(1, G))[::-1] + [0]:
        todo.append((0, run(load_values, k)))
        todo += [(0, run(scores_back, k, i)) for i in range(rows // QB)]
        todo.append((0, run(keys_back, k)))
        if k:
            todo.append((0, run(values_back, k)))
    todo.append((0, run(base_block, *base_blocks[0], False), (n_base, 0)))
    todo += [(0, run(d_ema, t)) for t in range(tiles)]
    todo += [(0, run(ends, t)) for t in range(tiles)]
    todo += [(0, exchange), (0, values_here)]
    for number, block in enumerate(value_blocks):
        todo.append((0, run(value_block, *block, number == 0), (n_value, block[0])))
    todo.append((0, carries))
    todo += [(0, run(back, t)) for t in range(tiles)]
    todo += [(0, lambda: begin(1)), (0, tile_x), (0, buckets, "small")]
    todo += [(0, run(correlate, t)) for t in range(tiles)]
    todo.append((0, share_sums, (len(grads) - 1, 0)))

    def needs(i):
        n, at, width = chunks[i]
        return (n, at) if n >= n_base else None

    steps = []
    for i in range(min(LEAD, total)):
        steps.append((run(stage_core, i), needs(i)))
    steps.append(lambda: begin(0))
    for turn in range(total + 3 * LAG):
        for what, lag in ((stage_four, 3), (stage_three, 2), (stage_two, 1), (stage_one, 0)):
            if 0 <= turn - lag * LAG < total:
                steps.append(run(what, turn - lag * LAG))
        if turn + LEAD < total:
            steps.append((run(stage_core, turn + LEAD), needs(turn + LEAD)))
        if turn >= total:
            late = turn - total
            moves = ([wire.to(y, 1 - c, z, x)], xs, ys, zs)
            if late < 4:
                steps.append((run(small_stage, moves[late]), "small"))
    interleave(steps, todo, MOST)
    small_out[...] = small_acc[...]
    wait(0)
    wait(1)
    wire.finish()


LEAD = 3
MOST = 1


def dot_t(a, b):
    return lax.dot_general(a, b, (((0,), (0,)), ((), ())), preferred_element_type=F32)


def bucket_sums(length, bucket_count, strip):
    edges = bucket_edges(bucket_count)
    lag0 = lax.broadcasted_iota(jnp.int32, (QB, LANES), 0) - lax.broadcasted_iota(
        jnp.int32, (QB, LANES), 1
    )
    totals = [jnp.zeros((1, LANES), F32) for k in range(bucket_count)]
    for t in range((length + QB) // LANES):
        base = length - t * LANES
        low, high = base - LANES + 1, base + QB - 1
        if high < 0:
            continue
        value = strip[:, t * LANES : (t + 1) * LANES]
        for k in range(bucket_count):
            top = edges[k + 1] if k + 1 < bucket_count else length
            if edges[k] <= high and top > low:
                lag = lag0 + base
                inside = (lag >= edges[k]) & (lag < top)
                totals[k] = totals[k] + jnp.sum(jnp.where(inside, value, 0.0), axis=0, keepdims=True)
    return totals


def backward_all(lay, H, NB, grads, fulls, values, share):
    X, Y, Z, G = lay.X, lay.Y, lay.Z, lay.G
    R, V = values["d_att"].shape
    D = values["pre"].shape[1]
    T, zw = D // LANES, values["queries"].shape[1]
    rows = R // lay.BL
    micro = lay.MS // lay.items
    shapes = [grad.shape[-2:] for grad in grads] + [full.shape[-2:] for full in fulls] + [(share, LANES)]
    kinds = [grad.dtype for grad in grads] + [BF16, BF16, F32]
    known = len(grads)
    chunks = chunks_of([shape for shape in shapes[:known]], share * LIMIT)
    base_blocks = column_blocks(shapes[known][1])
    chunks += [(known,) + block for block in base_blocks[1:]]
    chunks += [(known,) + base_blocks[0]]
    chunks += [(known + 1,) + block for block in column_blocks(shapes[known + 1][1])]
    chunks += [(known + 2, 0, LANES)]
    scratch = []
    for n, at, cols in chunks:
        r = shapes[n][0]
        left = half_columns(cols)
        right = cols - left if cols > left else LANES
        kind = kinds[n]
        scratch += [
            pltpu.VMEM((Y, Z, X, r, cols), kind),
            pltpu.VMEM((X - 1, Y, Z, r, left), kind),
            pltpu.VMEM((Y - 1, Z, X, r, right), kind),
            pltpu.VMEM((Y - 1, Z, r, left), kind),
            pltpu.VMEM((X - 1, Z, r, right), kind),
            pltpu.VMEM((Z - 1, r, cols), kind),
        ]
    hops = 1 + (X - 1) + (Y - 1) + (Z - 1)
    per = 1 + 2 * (X - 1 + Y - 1) + Z - 1
    small = (8, LANES)
    outs = [jax.ShapeDtypeStruct(shape, F32) for shape in shapes]
    outs.append(jax.ShapeDtypeStruct(small, F32))
    outs += [jax.ShapeDtypeStruct((micro, lay.items, rows, D), BF16)] * 2
    outs += [jax.ShapeDtypeStruct(full.shape, BF16) for full in fulls]
    outs += [jax.ShapeDtypeStruct((G - 1, R, V), BF16)] * 2
    scratch += [pltpu.VMEM(small, F32), pltpu.VMEM((hops,) + small, F32)]
    heights = sorted({shapes[n][0] for n, at, width in chunks})
    widest = {r: max(w for n, at, w in chunks if shapes[n][0] == r) for r in heights}
    scratch += [
        pltpu.SemaphoreType.DMA((len(chunks) * per + hops,)),
        pltpu.SemaphoreType.DMA((len(chunks) * per + hops,)),
        pltpu.SemaphoreType.DMA((len(chunks),)),
        pltpu.SemaphoreType.DMA((2, lay.BL)),
        pltpu.SemaphoreType.DMA((2, lay.MS)),
        pltpu.SemaphoreType.DMA((2,)),
        pltpu.VMEM((T, R, LANES), F32),
        pltpu.VMEM((T, R, LANES), F32),
        pltpu.VMEM((T, R, LANES), F32),
        pltpu.VMEM((T, LANES, LANES), F32),
        pltpu.VMEM((D, LANES), F32),
        pltpu.VMEM((Y, 2, Z, X, share, LANES), F32),
        pltpu.VMEM((T, H, SEG, LANES), F32),
        pltpu.VMEM((T, H, LANES), F32),
        pltpu.VMEM((G - 1, T, H, LANES), F32),
        pltpu.VMEM((T, H, LANES), F32),
        pltpu.VMEM((lay.BL, rows, D), BF16),
        pltpu.SemaphoreType.DMA((3, G - 1)),
        pltpu.SemaphoreType.DMA((3, G - 1)),
        pltpu.VMEM((Y, 2, Z, X, share, 768), BF16),
        pltpu.VMEM((R, V), BF16),
        pltpu.VMEM((R, 768), BF16),
        pltpu.VMEM((R, 768), F32),
        pltpu.VMEM((R, R), BF16),
        pltpu.VMEM((QB, (G + 1) * R), F32),
        pltpu.VMEM((R, zw), F32),
        pltpu.VMEM((G - 1, R, zw), BF16),
        pltpu.VMEM((G - 1, R, zw), BF16),
        pltpu.VMEM((R, zw), BF16),
        pltpu.VMEM((R, 768), BF16),
        pltpu.VMEM((R, D), F32),
        pltpu.VMEM((R, D), F32),
        pltpu.SemaphoreType.DMA,
    ]
    scratch += [pltpu.VMEM((2, Y, Z, X, r, widest[r]), BF16) for r in heights]
    order = (
        ("x_blocks", VM), ("d_in", ANY), ("d_att", VM), ("delta", VM), ("queries", VM), ("keys", VM),
        ("vals", ANY), ("probs", VM), ("z_pre", VM), ("gains_small", VM), ("mixed", VM), ("ema", VM),
        ("base_rest", ANY), ("value_pre", ANY), ("w_base", ANY), ("w_value", ANY), ("pre", ANY),
        ("gains", VM), ("table", VM), ("turned", VM), ("si", VM), ("ri", VM), ("block_out", ANY),
    )
    values = dict(values, w_base=fulls[0], w_value=fulls[1])
    order = tuple(item for item in order if item[0] != "d_in")

    def body(*refs):
        named = refs[known : known + len(order)]
        ins = (tuple(refs[:known]), named[0], None) + tuple(named[1:])
        rest = refs[known + len(order) :]
        results, small_out, moved = rest[: known + 3], rest[known + 3], rest[known + 4 : known + 6]
        made, dvo, dvi = rest[known + 6 : known + 8], rest[known + 8], rest[known + 9]
        scatter_kernel(
            lay, H, NB, chunks, ins, (results, small_out, moved, tuple(made), dvo, dvi), rest[known + 10 :]
        )

    result = pl.pallas_call(
        body,
        out_shape=outs,
        in_specs=[ANY] * known + [spec for name, spec in order],
        out_specs=[VM] * (known + 4) + [ANY] * 6,
        scratch_shapes=scratch,
        compiler_params=pltpu.CompilerParams(
            collective_id=1, has_side_effects=True, vmem_limit_bytes=60 * 2**20
        ),
        name="backward_all",
    )(*grads, *[values[name] for name, spec in order])
    return result[: known + 3], result[known + 3], result[known + 4 : known + 6]


def row(ref, index, lanes):
    return jnp.broadcast_to(ref[pl.ds(index, 1), lanes], (SEG, LANES))


def lane_call(kernel, outs, args, name):
    def spec(a):
        lead = len(a.shape) - 1
        return pl.BlockSpec(a.shape[:-1] + (LANES,), lambda i: (0,) * lead + (i,))

    return pl.pallas_call(
        kernel,
        out_shape=outs,
        grid=(args[0].shape[-1] // LANES,),
        in_specs=[spec(a) for a in args],
        out_specs=jax.tree.map(spec, outs),
        compiler_params=pltpu.CompilerParams(vmem_limit_bytes=32 * 2**20),
        name=name,
    )(*args)


def shifted(value, by):
    where = lax.broadcasted_iota(jnp.int32, (SEG, LANES), 0)
    if by > 0:
        return jnp.where(where >= by, pltpu.roll(value, by, 0), 0.0)
    return jnp.where(where < SEG + by, pltpu.roll(value, SEG + by, 0), 0.0)


def ema_ends_kernel(H, x_ref, tab_ref, s_ref, r_ref):
    rows, width = x_ref.shape
    steps = rows // SEG

    def tile(lanes):
        decay = [row(tab_ref, h, lanes) for h in range(H)]

        def step(t, state):
            s, r = state
            xt = x_ref[pl.ds(t, SEG, stride=steps), lanes]
            r = tuple(decay[h] * r[h] + s[h] for h in range(H))
            s = tuple(decay[h] * s[h] + xt for h in range(H))
            return s, r

        zero = tuple(tab_ref[0:SEG, lanes] * 0.0 for h in range(H))
        s, r = lax.fori_loop(0, steps, step, (zero, zero))
        for h in range(H):
            log = row(tab_ref, H + h, lanes)
            sh, rh = s[h], r[h]
            for d in (1, 2, 4):
                span = d * steps
                sd, rd = shifted(sh, d), shifted(rh, d)
                power = jnp.exp(span * log)
                rh = rh + power * rd + (span * jnp.exp((span - 1) * log)) * sd
                sh = sh + power * sd
            s_ref[h, :, lanes] = sh
            r_ref[h, :, lanes] = rh

    tile(slice(None))


def ema_out_kernel(H, x_ref, tab_ref, omega_ref, s_ref, r_ref, inc_ref, ema_ref, si_ref, ri_ref):
    rows, width = x_ref.shape
    steps = rows // SEG

    def tile(lanes):
        decay = [row(tab_ref, h, lanes) for h in range(H)]
        gain = [row(tab_ref, 2 * H + h, lanes) for h in range(H)]
        omega = row(omega_ref, 0, lanes)
        start = []
        span = (lax.broadcasted_iota(jnp.int32, (SEG, LANES), 0) * steps).astype(F32)
        for h in range(H):
            log = row(tab_ref, H + h, lanes)
            s_dev = row(inc_ref, h, lanes)
            r_dev = row(inc_ref, H + h, lanes)
            power = jnp.exp(span * log)
            s_in = shifted(s_ref[h, :, lanes], 1) + power * s_dev
            r_in = (
                shifted(r_ref[h, :, lanes], 1)
                + power * r_dev
                + (span * jnp.exp((span - 1.0) * log)) * s_dev
            )
            si_ref[h, :, lanes] = s_in
            ri_ref[h, :, lanes] = r_in
            start.append(s_in)

        def step(t, s):
            xt = x_ref[pl.ds(t, SEG, stride=steps), lanes]
            s = tuple(decay[h] * s[h] + xt for h in range(H))
            parts = [gain[h] * s[h] for h in range(H)]
            while len(parts) > 1:
                parts = [parts[i] + parts[i + 1] for i in range(0, len(parts), 2)]
            ema_ref[pl.ds(t, SEG, stride=steps), lanes] = parts[0] + omega * xt
            return s

        lax.fori_loop(0, steps, step, tuple(start))

    tile(slice(None))


def ema_back_ends_kernel(H, d_ref, tab_ref, l_ref):
    rows, width = d_ref.shape
    steps = rows // SEG

    def tile(lanes):
        decay = [row(tab_ref, h, lanes) for h in range(H)]

        def step(i, lam):
            dt = d_ref[pl.ds(steps - 1 - i, SEG, stride=steps), lanes]
            return tuple(decay[h] * lam[h] + dt for h in range(H))

        zero = tuple(tab_ref[0:SEG, lanes] * 0.0 for h in range(H))
        lam = lax.fori_loop(0, steps, step, zero)
        for h in range(H):
            log = row(tab_ref, H + h, lanes)
            lh = lam[h]
            for d in (1, 2, 4):
                lh = lh + jnp.exp(d * steps * log) * shifted(lh, -d)
            l_ref[h, :, lanes] = lh

    tile(slice(None))


def ema_sums_kernel(H, x_ref, d_ref, tab_ref, si_ref, ri_ref, out_ref):
    rows, width = x_ref.shape
    steps = rows // SEG
    group = H // 2

    def tile(lanes):
        for first in range(0, H, group):
            decay = [row(tab_ref, first + h, lanes) for h in range(group)]

            def step(t, state):
                s, r, c, q, o = state
                xt = x_ref[pl.ds(t, SEG, stride=steps), lanes]
                dt = d_ref[pl.ds(t, SEG, stride=steps), lanes]
                r = tuple(decay[h] * r[h] + s[h] for h in range(group))
                s = tuple(decay[h] * s[h] + xt for h in range(group))
                c = tuple(c[h] + dt * s[h] for h in range(group))
                q = tuple(q[h] + dt * r[h] for h in range(group))
                return s, r, c, q, o + dt * xt

            zero = tuple(tab_ref[0:SEG, lanes] * 0.0 for h in range(group))
            s = tuple(si_ref[first + h, :, lanes] for h in range(group))
            r = tuple(ri_ref[first + h, :, lanes] for h in range(group))
            s, r, c, q, o = lax.fori_loop(0, steps, step, (s, r, zero, zero, zero[0]))
            for h in range(group):
                out_ref[pl.ds(first + h, 1), lanes] = jnp.sum(c[h], axis=0, keepdims=True)
                out_ref[pl.ds(H + first + h, 1), lanes] = jnp.sum(q[h], axis=0, keepdims=True)
            out_ref[pl.ds(2 * H, 1), lanes] = jnp.sum(o, axis=0, keepdims=True)

    tile(slice(None))


def ema_back_kernel(H, d_ref, tab_ref, omega_ref, l_ref, inc_ref, dx_ref):
    rows, width = d_ref.shape
    steps = rows // SEG

    def tile(lanes):
        decay = [row(tab_ref, h, lanes) for h in range(H)]
        gain = [row(tab_ref, 2 * H + h, lanes) for h in range(H)]
        omega = row(omega_ref, 0, lanes)
        start = []
        span = ((SEG - 1 - lax.broadcasted_iota(jnp.int32, (SEG, LANES), 0)) * steps).astype(F32)
        for h in range(H):
            log = row(tab_ref, H + h, lanes)
            l_dev = row(inc_ref, h, lanes)
            start.append(shifted(l_ref[h, :, lanes], -1) + jnp.exp(span * log) * l_dev)

        def step(i, lam):
            at = pl.ds(steps - 1 - i, SEG, stride=steps)
            dt = d_ref[at, lanes]
            lam = tuple(decay[h] * lam[h] + dt for h in range(H))
            parts = [gain[h] * lam[h] for h in range(H)]
            while len(parts) > 1:
                parts = [parts[i] + parts[i + 1] for i in range(0, len(parts), 2)]
            dx_ref[at, lanes] = parts[0] + omega * dt
            return lam

        lax.fori_loop(0, steps, step, tuple(start))

    tile(slice(None))


def call(kernel, outs, args, specs=None, scratch=(), vmem=58, name=None):
    return pl.pallas_call(
        kernel,
        out_shape=outs,
        in_specs=specs or [VM] * len(args),
        out_specs=jax.tree.map(lambda o: VM, outs),
        scratch_shapes=list(scratch),
        compiler_params=pltpu.CompilerParams(vmem_limit_bytes=vmem * 2**20),
        name=name,
    )(*args)


QB = 256
STRETCH = 128


def bias_kernel(length, bucket_count, bias_ref, strip_ref):
    edges = bucket_edges(bucket_count)
    tiles = length // LANES + QB // LANES
    lag0 = lax.broadcasted_iota(jnp.int32, (QB, LANES), 0) - lax.broadcasted_iota(
        jnp.int32, (QB, LANES), 1
    )
    for t in range(strip_ref.shape[1] // LANES):
        base = length - t * LANES
        low, high = base - LANES + 1, base + QB - 1
        start = max([k for k in range(bucket_count) if edges[k] <= low], default=0)
        value = jnp.full((QB, LANES), bias_ref[start], F32)
        for k in range(start + 1, bucket_count):
            if edges[k] <= high:
                value = jnp.where(lag0 + base >= edges[k], bias_ref[k], value)
        strip_ref[:, t * LANES : (t + 1) * LANES] = value


def attend_body(lay, g, far, q_ref, strip_ref, keys, vals, att_ref, probs_ref, scores, part):
    G = lay.G
    rows, zw = q_ref.shape
    length = G * rows
    r0 = lax.broadcasted_iota(jnp.int32, (QB, rows), 0)
    c0 = lax.broadcasted_iota(jnp.int32, (QB, rows), 1)

    def one(i, carry):
        at = i * QB
        q = q_ref[pl.ds(at, QB), :]
        for k in range(G):
            owner = lax.rem(g - k + G, G)
            s = mm_t(q, keys[k])
            off = jnp.clip(length - rows * (g - owner) - at, 0, length)
            s = s * (zw ** (-0.5)) + strip_ref[:, pl.ds(pl.multiple_of(off, LANES), rows)]
            if k == 0:
                pos = r0 + at
                s = jnp.where(pos // STRETCH == c0 // STRETCH, s, s + far)
                s = jnp.where(c0 <= pos, s, masked_fill)
            else:
                s = s + jnp.where(k <= g, far, masked_fill)
            scores[:, k * rows : (k + 1) * rows] = s
        s = scores[...]
        p = jnp.exp(s - jnp.max(s, axis=1, keepdims=True))
        p = p * (1.0 / jnp.sum(p, axis=1, keepdims=True))
        total = jnp.zeros((QB, att_ref.shape[1]), F32)
        for k in range(G):
            low = p[:, k * rows : (k + 1) * rows].astype(BF16)
            probs_ref[k, pl.ds(at, QB), :] = low
            total += mm(low, vals[k])
        att_ref[pl.ds(at, QB), :] = total
        return carry

    one(part, 0)


def attend_back_kernel(lay, bucket_count, flag_ref, q_ref, da_ref, delta_ref, probs_ref, *refs):
    G = lay.G
    keys, vals, dq_ref, dk_ref, dv_ref, dko_ref, dvo_ref, bucket_ref, strip, ds_ref = refs
    rows, zw = q_ref.shape
    length = G * rows
    g = flag_ref[1]
    scale = zw ** (-0.5)
    edges = bucket_edges(bucket_count)
    strip[...] = jnp.zeros(strip.shape, F32)

    def one(i, carry):
        at = pl.multiple_of(i * QB, QB)
        da = da_ref[pl.ds(at, QB), :]
        dq = jnp.zeros((QB, zw), F32)
        for k in range(G):
            owner = lax.rem(g - k + G, G)
            dw = mm_t(da, vals[k])
            p = probs_ref[k, pl.ds(at, QB), :].astype(F32)
            ds = p * (dw - delta_ref[pl.ds(at, QB), :])
            off = jnp.clip(length - rows * (g - owner) - at, 0, length)
            strip[:, pl.ds(pl.multiple_of(off, LANES), rows)] += ds
            low = ds.astype(BF16)
            dq += mm(low, keys[k])
            ds_ref[k, pl.ds(at, QB), :] = low
        dq_ref[pl.ds(at, QB), :] = dq * scale
        return carry

    lax.fori_loop(0, rows // QB, one, 0)
    for k in range(G):
        dk = lax.dot_general(
            ds_ref[k], q_ref[...], (((0,), (0,)), ((), ())), preferred_element_type=F32
        )
        dv = lax.dot_general(
            probs_ref[k], da_ref[...], (((0,), (0,)), ((), ())), preferred_element_type=F32
        )
        if k == 0:
            dk_ref[...] = dk * scale
            dv_ref[...] = dv
        else:
            dko_ref[k - 1] = (dk * scale).astype(BF16)
            dvo_ref[k - 1] = dv.astype(BF16)
    lag0 = lax.broadcasted_iota(jnp.int32, (QB, LANES), 0) - lax.broadcasted_iota(
        jnp.int32, (QB, LANES), 1
    )
    sums = [jnp.zeros((1, LANES), F32) for k in range(bucket_count)]
    for t in range((length + QB) // LANES):
        base = length - t * LANES
        low, high = base - LANES + 1, base + QB - 1
        if high < 0:
            continue
        value = strip[:, t * LANES : (t + 1) * LANES]
        for k in range(bucket_count):
            top = edges[k + 1] if k + 1 < bucket_count else length
            if edges[k] <= high and top > low:
                lag = lag0 + base
                inside = (lag >= edges[k]) & (lag < top)
                sums[k] = sums[k] + jnp.sum(jnp.where(inside, value, 0.0), axis=0, keepdims=True)
    for k in range(bucket_count):
        bucket_ref[pl.ds(k, 1), :] = sums[k]


def silu_slope(values):
    gate_value = jax.nn.sigmoid(values)
    return gate_value * (1.0 + values * (1.0 - gate_value))


def normalize(seq_rows):
    centered = seq_rows - jnp.mean(seq_rows, axis=-1, keepdims=True)
    inverse = lax.rsqrt(jnp.mean(centered * centered, axis=-1, keepdims=True) + epsilon)
    return (centered * inverse, inverse)


def normalize_back(grad_scaled, unit_rows, inverse):
    return inverse * (
        grad_scaled
        - jnp.mean(grad_scaled, axis=-1, keepdims=True)
        - unit_rows * jnp.mean(grad_scaled * unit_rows, axis=-1, keepdims=True)
    )


def mm(a, b):
    return jnp.dot(a, b, preferred_element_type=F32)


def mm_t(a, b):
    return lax.dot_general(a, b, (((1,), (1,)), ((), ())), preferred_element_type=F32)


def wgrad(a, b):
    return lax.dot_general(a, b, (((0,), (0,)), ((), ())), preferred_element_type=F32).astype(BF16)


def shards(
    lay,
    tokens,
    cotangent,
    stretch_size,
    w_value,
    w_base,
    w_out,
    w_up,
    w_down,
    ema_delta,
    ema_alpha,
    ema_beta,
    ema_gamma,
    ema_omega,
    first_gain,
    second_gain,
    query_gain,
    query_bias,
    key_gain,
    relative_bias,
):
    micro, items, seq_len, D = tokens.shape
    H = ema_delta.shape[1]
    zw = query_gain.shape[0]
    V = w_value.shape[1]
    NB = relative_bias.shape[0]
    length = seq_len * lay.S
    G = lay.G
    R = lay.BL * seq_len
    d_at, b_at = lax.axis_index("dp"), lax.axis_index("seq")
    c_at, y_at = d_at % 2, d_at // 2
    q_at = b_at // lay.Cq
    g_at = (b_at % lay.Cq) * 2 + c_at
    share = ema_delta.shape[0]

    def group_perm(k):
        pairs = []
        for y in range(lay.Y):
            for q in range(lay.Q):
                for g in range(G):
                    t = (g + k) % G
                    src = (y * 2 + g % 2) * lay.S + q * lay.Cq + g // 2
                    dst = (y * 2 + t % 2) * lay.S + q * lay.Cq + t // 2
                    pairs.append((src, dst))
        return pairs

    def shift(value, k):
        return lax.ppermute(value, ("dp", "seq"), group_perm(k % G))

    marks = jnp.broadcast_to(
        stretch_size.reshape(1, -1).astype(BF16), (share, lay.MS)
    )
    used = 4 * H + 3 + lay.MS
    pack = jnp.concatenate(
        [
            ema_delta,
            ema_alpha,
            ema_beta,
            ema_gamma,
            ema_omega[:, None],
            first_gain[:, None],
            second_gain[:, None],
            marks,
            jnp.zeros((share, LANES - used), BF16),
        ],
        1,
    )
    x_blocks, cot_blocks, fulls, rest = forward_all(
        lay, H, tokens, cotangent, (pack, w_value, w_base, w_out, w_up, w_down),
        query_gain[None], query_bias[None], key_gain[None], relative_bias,
    )
    mixed, ema_tiles, s_in, r_in, table, turned = rest[:6]
    value_pre, base, queries, keys_all, vals_all, probs, attended = rest[6:]
    flags = jnp.stack([g_at, g_at])
    mats = [full.reshape(-1, full.shape[-1]) for full in fulls[1:]]
    mat_value, mat_base, mat_out, mat_up, mat_down = mats
    gain_first = turned[:, 4 * H + 1].reshape(D)
    gain_second = turned[:, 4 * H + 2].reshape(D)

    x_low = x_blocks.reshape(R, D)
    x = x_low.astype(F32)
    grad_out = cot_blocks.reshape(R, D).astype(F32)

    z_pre = base[:, :zw]
    reset_pre = base[:, zw : zw + V]
    cand_pre = base[:, zw + V : zw + V + D]
    update_pre = base[:, zw + V + D :]
    reset_gate = jax.nn.silu(reset_pre)
    update = jax.nn.sigmoid(update_pre)
    gated = (attended * reset_gate).astype(BF16)
    cand_in = cand_pre + mm(gated, mat_out)
    candidate = jax.nn.silu(cand_in)
    first_sum = x + update * (candidate - x)
    unit_first, inverse_first = normalize(first_sum)
    normed = unit_first * gain_first
    normed_low = normed.astype(BF16)
    hidden_pre = mm(normed_low, mat_up)
    hidden = jax.nn.silu(hidden_pre).astype(BF16)
    second_sum = normed + mm(hidden, mat_down)
    unit_second, inverse_second = normalize(second_sum)
    block_out = (unit_second * gain_second).astype(BF16)

    grad_gain_second = jnp.sum(grad_out * unit_second, axis=0)
    grad_second = normalize_back(grad_out * gain_second, unit_second, inverse_second)
    branch = grad_second.astype(BF16)
    grad_mat_down = wgrad(hidden, branch)
    hidden_grad = (mm_t(branch, mat_down) * silu_slope(hidden_pre)).astype(BF16)
    grad_mat_up = wgrad(normed_low, hidden_grad)
    grad_normed = grad_second + mm_t(hidden_grad, mat_up)
    grad_gain_first = jnp.sum(grad_normed * unit_first, axis=0)
    grad_first = normalize_back(grad_normed * gain_first, unit_first, inverse_first)
    cand_low = (grad_first * update * silu_slope(cand_in)).astype(BF16)
    grad_mat_out = wgrad(gated, cand_low)
    grad_gated = mm_t(cand_low, mat_out)
    att_low = (grad_gated * reset_gate).astype(BF16)
    grad_reset = grad_gated * attended * silu_slope(reset_pre)
    grad_update = grad_first * (candidate - x) * update * (1.0 - update)
    delta = jnp.sum(att_low.astype(F32) * attended, axis=1, keepdims=True)
    base_rest = jnp.concatenate(
        [grad_reset.astype(BF16), cand_low, grad_update.astype(BF16)], 1
    )
    pre = grad_first * (1.0 - update)
    gains = jnp.concatenate(
        [grad_gain_first[None], grad_gain_second[None], jnp.zeros((6, D), F32)]
    )
    shape = (lay.Y, 2, lay.Z, lay.X)

    def split(grad):
        return grad.reshape(shape + (-1, grad.shape[-1]))

    reduced, small_total, moved = backward_all(
        lay,
        H,
        NB,
        [split(grad_mat_down), split(grad_mat_up), split(grad_mat_out)],
        [fulls[2], fulls[1]],
        dict(
            x_blocks=x_blocks, d_att=att_low, delta=delta, queries=queries, keys=keys_all,
            vals=vals_all, probs=probs, z_pre=z_pre,
            gains_small=jnp.concatenate([query_gain[None], key_gain[None], jnp.zeros((6, zw), F32)]),
            mixed=mixed, ema=ema_tiles, base_rest=base_rest, value_pre=value_pre, pre=pre, gains=gains,
            table=table, turned=turned, si=s_in, ri=r_in,
            block_out=block_out.reshape(lay.BL, seq_len, D),
        ),
        share,
    )
    own = reduced[5]
    corr, lagged = own[:, :H], own[:, H : 2 * H]
    p = jax.nn.sigmoid(ema_delta.astype(F32))
    a = jax.nn.sigmoid(ema_alpha.astype(F32))
    beta = ema_beta.astype(F32)
    read = ema_gamma.astype(F32) * (H ** (-0.5))
    q_grad = read * p * beta * lagged
    return (
        moved[0],
        moved[1].astype(F32),
        reduced[4],
        reduced[3],
        reduced[2],
        reduced[1],
        reduced[0],
        (read * beta * corr - a * q_grad) * p * (1.0 - p),
        -p * q_grad * a * (1.0 - a),
        p * read * corr,
        p * beta * corr * (H ** (-0.5)),
        own[:, 2 * H],
        own[:, 2 * H + 1],
        own[:, 2 * H + 2],
        small_total[0, :zw],
        small_total[1, :zw],
        small_total[2, :zw],
        small_total[3, :NB],
    )


def solution(mesh):
    rows = P(None, "dp", "seq", None)
    part2, part1 = P(("dp", "seq"), None), P(("dp", "seq"))
    in_specs = (rows, rows, P(None, "dp")) + (part2,) * 9 + (part1,) * 3 + (P(),) * 4
    out_specs = (rows, rows) + (part2,) * 9 + (part1,) * 3 + (P(),) * 4

    def whole(tokens, *rest):
        micro, seqs = tokens.shape[:2]
        lay = Layout(mesh.shape["dp"], mesh.shape["seq"], micro, seqs // mesh.shape["dp"])
        return jax.shard_map(
            functools.partial(shards, lay),
            mesh=mesh,
            in_specs=in_specs,
            out_specs=out_specs,
            check_vma=False,
        )(tokens, *rest)

    return whole
```

profile of v0, /device:TPU:0, one launch (start us, length us, event | category | flops | bytes accessed | tf_op | source)
XLA Modules:
  0.0 327.1 jit_solution(16776078975796005569)
XLA Ops:
  0.7 0.8 copy.68
  1.4 0.8 copy.69
  2.2 0.8 copy.70
  3.7 0.8 copy.71
  4.5 0.7 copy.72
  5.2 0.7 copy.73
  6.0 0.7 copy.74
  6.7 0.7 concatenate.12.refs_2_
  7.4 117.3 %forward_all.1 = (bf16[4,128,768]{2,1,0:T(8,128)(2,1)}, bf16[4,128,768]{2,1,0:T(8,128)(2,1)}, bf16[2,2,4,2,24,128]{5,4,3,2,1,0:T(8,128)(2,1)}, bf16[2,2,4,2,24,1...) custom-call(bf16[2,2,128,768]{3,2,1,0:T(8,128)(2,1)} %refs_0_.1, ...), custom_call_target="tpu_custom_call" | custom-call | tf_op jit(solution)/shard_map/forward_all/pallas_call | solution.py:649
  124.8 3.9 %multiply_convert_fusion.3 = bf16[512,1536]{1,0:T(8,128)(2,1)S(1)} fusion(f32[512,1536]{1,0:T(8,128)} %get-tuple-element.49, f32[512,3200]{1,0:T(8,128)} %get-tuple-element.48), kind=kLoop, calls=%fused_computation.10 | loop fusion | flops 4718592 | bytes 7864320 | tf_op jit(solution)/shard_map/convert_element_type | solution.py:1673
  128.7 0.8 copy-done.1
  129.7 3.9 %fusion.19 = (f32[512]{0:T(512)S(1)}, f32[512,768]{1,0:T(8,128)S(1)}, f32[512,768]{1,0:T(8,128)S(1)}) fusion(f32[512,3200]{1,0:T(8,128)S(1)} %copy-done.1, bf16[4,128,768]{2,1,0:T(8,128)(2,1)S(1)} %copy-done.3, bf16[512,1536]{1,0:T(8,128)(2,1)S(1)} %multiply_convert_fusion.3, bf16[1536,768]{1,0:T(8,128)(2,1)} %bitcast.83), kind=kOutput, calls=%fused_computation.81 | convolution fusion | flops 1213070848 | bytes 11012096 | tf_op jit(solution)/shard_map/dot_general | solution.py:1572
  133.9 0.8 slice_reduce_fusion.3
  134.8 1.5 fusion.18
  136.4 2.1 fusion.20
  138.8 0.8 copy-done
  139.6 1.6 fusion.8
  142.0 1.9 fusion.1
  143.9 1.8 multiply_reduce_fusion.1
  146.5 2.9 multiply_convert_fusion.5
  149.4 3.5 %multiply_reduce_fusion = (f32[512]{0:T(512)S(1)}, bf16[512,1536]{1,0:T(8,128)(2,1)}, bf16[512,1536]{1,0:T(8,128)(2,1)S(1)}) fusion(f32[512,1536]{1,0:T(8,128)S(1)} %copy-done.2, f32[512,3200]{1,0:T(8,128)S(1)} %copy-done.1, bf16[512,768]{1,0:T(8,128)(2,1)S(1)} %get-tuple-element.146, bf16[1536,768]{1,0:T(8,128)(2,1)S(1)} %bitcast.84), kind=kOutput, calls=%fused_computation.6 | convolution fusion | flops 1220541952 | bytes 12584960 | tf_op jit(solution)/shard_map/dot_general | solution.py:1576
  152.9 2.1 pad_maximum_fusion.refs_14_
  155.0 0.9 copy.75.refs_5_
  155.8 4.4 %convolution_convert_fusion = bf16[1536,768]{1,0:T(8,128)(2,1)} fusion(bf16[512,1536]{1,0:T(8,128)(2,1)} %copy-done.6, bf16[512,768]{1,0:T(8,128)(2,1)S(1)} %get-tuple-element.146), kind=kOutput, calls=%fused_computation | convolution fusion | flops 1209139200 | bytes 4718592 | tf_op jit(solution)/shard_map/dot_general | solution.py:1580
  160.3 3.1 convolution_convert_fusion.1
  163.3 2.9 convolution_convert_fusion.2
  166.3 1.7 slice.50.refs_10_
  168.6 146.6 %backward_all.1 = (f32[48,768]{1,0:T(8,128)}, f32[24,1536]{1,0:T(8,128)}, f32[48,768]{1,0:T(8,128)}, f32[24,3200]{1,0:T(8,128)}, f32[24,1536]{1,0:T(8,128)}, /*i...) custom-call(bf16[2,2,4,2,48,768]{5,4,3,2,1,0:T(8,128)(2,1)} %bitcast, ...), custom_call_target="tpu_custom_call" | custom-call | tf_op jit(solution)/shard_map/backward_all/pallas_call | solution.py:1227
  315.3 2.5 convert_element_type.104
  320.6 0.7 slice_reduce_fusion
  322.4 0.9 copy.90
  323.9 0.7 copy.92
  (81 shorter events, 10.5 us)
Async XLA Ops:
  124.8 4.7 %copy-start.1 = (f32[512,3200]{1,0:T(8,128)S(1)}, f32[512,3200]{1,0:T(8,128)}, u32[]{:S(2)}) copy-start(f32[512,3200]{1,0:T(8,128)} %get-tuple-element.48) | copy-start | bytes 19660804
  124.8 4.9 %copy-start.3 = (bf16[4,128,768]{2,1,0:T(8,128)(2,1)S(1)}, bf16[4,128,768]{2,1,0:T(8,128)(2,1)}, u32[]{:S(2)}) copy-start(bf16[4,128,768]{2,1,0:T(8,128)(2,1)} %get-tuple-element.47.refs_3_) | copy-start | bytes 2359300
  128.7 4.9 %copy-start.6 = (bf16[512,1536]{1,0:T(8,128)(2,1)}, bf16[512,1536]{1,0:T(8,128)(2,1)S(1)}, u32[]{:S(2)}) copy-start(bf16[512,1536]{1,0:T(8,128)(2,1)S(1)} %multiply_convert_fusion.3) | copy-start | bytes 4718596
  129.7 5.0 %copy-start.19 = (bf16[2,2,4,2,24,1536]{5,4,3,2,1,0:T(8,128)(2,1)S(1)}, bf16[2,2,4,2,24,1536]{5,4,3,2,1,0:T(8,128)(2,1)}, u32[]{:S(2)}) copy-start(bf16[2,2,4,2,24,1536]{5,4,3,2,1,0:T(8,128)(2,1)} %get-tuple-element.52) | copy-start | bytes 7077892
  134.7 1.7 copy-start.20
  136.3 5.7 %copy-start.21 = (f32[512,1536]{1,0:T(8,128)}, f32[512,1536]{1,0:T(8,128)S(1)}, u32[]{:S(2)}) copy-start(f32[512,1536]{1,0:T(8,128)S(1)} %fusion.18) | copy-start | bytes 9437188
  138.5 1.1 copy-start
  142.0 1.9 copy-start.4
  143.9 1.8 copy-start.23
  146.5 2.9 copy-start.2
  146.5 2.9 copy-start.18
  155.8 4.4 %copy-start.24 = (bf16[512,1536]{1,0:T(8,128)(2,1)S(1)}, bf16[512,1536]{1,0:T(8,128)(2,1)}, u32[]{:S(2)}) copy-start(bf16[512,1536]{1,0:T(8,128)(2,1)} %copy-done.23) | copy-start | bytes 4718596
  160.3 3.1 copy-start.5
  160.3 3.1 copy-start.22
  163.3 4.6 %copy-start.15 = (f32[128]{0:T(128)S(1)}, f32[128]{0:T(128)}, u32[]{:S(2)}) copy-start(f32[128]{0:T(128)} %param.34) | copy-start | bytes 1540
  163.3 4.6 %copy-start.16 = (f32[128]{0:T(128)S(1)}, f32[128]{0:T(128)}, u32[]{:S(2)}) copy-start(f32[128]{0:T(128)} %param.36) | copy-start | bytes 1540
  315.2 2.6 copy-start.14
  315.2 2.6 copy-start.9
  315.2 6.1 %copy-start.17 = (f32[8,128]{1,0:T(8,128)S(1)}, f32[8,128]{1,0:T(8,128)}, u32[]{:S(2)}) copy-start(f32[8,128]{1,0:T(8,128)} %get-tuple-element.75) | copy-start | bytes 12292
  315.3 7.1 %copy-start.7 = (bf16[2,2,128,768]{3,2,1,0:T(8,128)(2,1)S(1)}, bf16[2,2,128,768]{3,2,1,0:T(8,128)(2,1)}, u32[]{:S(2)}) copy-start(bf16[2,2,128,768]{3,2,1,0:T(8,128)(2,1)} %get-tuple-element.180) | copy-start | bytes 2359300
  315.3 8.0 %copy-start.13 = (f32[24,1536]{1,0:T(8,128)S(1)}, f32[24,1536]{1,0:T(8,128)}, u32[]{:S(2)}) copy-start(f32[24,1536]{1,0:T(8,128)} %get-tuple-element.182) | copy-start | bytes 442372
  317.8 6.2 %copy-start.8 = (f32[24,3200]{1,0:T(8,128)S(1)}, f32[24,3200]{1,0:T(8,128)}, u32[]{:S(2)}) copy-start(f32[24,3200]{1,0:T(8,128)} %get-tuple-element.183) | copy-start | bytes 921604
  317.8 6.9 %copy-start.12 = (f32[48,768]{1,0:T(8,128)S(1)}, f32[48,768]{1,0:T(8,128)}, u32[]{:S(2)}) copy-start(f32[48,768]{1,0:T(8,128)} %get-tuple-element.184) | copy-start | bytes 442372
  317.8 7.6 %copy-start.11 = (f32[24,1536]{1,0:T(8,128)S(1)}, f32[24,1536]{1,0:T(8,128)}, u32[]{:S(2)}) copy-start(f32[24,1536]{1,0:T(8,128)} %get-tuple-element.185) | copy-start | bytes 442372
  320.0 6.0 %copy-start.10 = (f32[48,768]{1,0:T(8,128)S(1)}, f32[48,768]{1,0:T(8,128)}, u32[]{:S(2)}) copy-start(f32[48,768]{1,0:T(8,128)} %get-tuple-element.186) | copy-start | bytes 442372
where the time goes:
time: 333 us; the launch traced here: 327 us
  Pallas kernels  264 us (79%)
  matrix products  25.1 us (8%)
  local copies, waits for them, and re-layouts  20.4 us (6%)
  other arithmetic  16.3 us (5%)
    pallas_call x1, Pallas kernels, backward_all(): pl.pallas_call(body, out_shape=outs, in_specs=[ANY] * known + [spec for n...  147 us
    pallas_call x1, Pallas kernels, forward_all(): pl.pallas_call(body, out_shape=outs, in_specs=[ANY] * (2 + count) + [VM]...  117 us
    unnamed x64, local copies, waits for them, and re-layouts  12 us
    dot_general x3, matrix products, wgrad(): lax.dot_general(a, b, (((0,), (0,)), ((), ())), preferred_element_type=F32)  10.4 us
    dot_general x3, matrix products, mm(): return jnp.dot(a, b, preferred_element_type=F32)  7.46 us
    dot_general x3, matrix products, mm_t(): lax.dot_general(a, b, (((1,), (1,)), ((), ())), preferred_element_type=F32)  7.2 us

commit v1 on v0

--- a/solution.py
+++ b/solution.py
@@ -690,8 +690,7 @@
             places.insert(0, i % extent)
             i = i // extent
         a, e = index(*places), extra_index(*places)
-        summed = total[a].astype(F32) + extra[e].astype(F32)
-        total[a] = summed.astype(total.dtype)
+        total[a] = total[a] + extra[e]
         return carry
 
     lax.fori_loop(0, size, one, 0)
@@ -705,9 +704,11 @@
     results, small_out, outs_to, made, dvo, dvi = outs
     bufs, own = scratch[: 6 * len(chunks)], scratch[6 * len(chunks) :]
     small_acc, small_recv, send, recv, local, t_send, t_recv, t_local = own[:8]
-    xt, dt, dx, sums, flat, split, l_end, mine, inbox, inc, gx, c_send, c_recv = own[8:21]
-    stage, vstage, bstage, pstage, ds, strip, dq, dko, dki, zlow, vlow, mixed_acc, x_acc, load = own[21:35]
-    halves = own[35:]
+    xt, dt, sums, flat, split, l_end, mine, inbox, inc, gx, c_send, c_recv = own[8:20]
+    dx = xt
+    stage, vstage, bstage, pstage, ds, strip, dq, dko, dki, zlow, mixed_acc, x_acc, load = own[20:33]
+    gstage, mixed_t, loads = own[33:36]
+    halves = own[36:]
     grads = grads + made + (split,)
     y, c, z, x, b = lay.here()
     X, Y, Z = lay.X, lay.Y, lay.Z
@@ -741,8 +742,17 @@
         room = [h for h in halves if h.shape[4] == r][0]
         return room.at[i % 2, :, :, :, :, pl.ds(0, width)]
 
+    def prefetch_half(i):
+        near = own_half(i) if i < total else None
+        if near is not None:
+            near.start()
+
     def stage_core(i):
         n, at, width = chunks[i]
+        if n_base <= n < n_base + 2:
+            settle()
+        if i == 0:
+            prefetch_half(0)
         arrived[i]["core"] = wire.start(
             grads[n].at[:, 1 - c, :, :, :, pl.ds(at, width)],
             buf(i, "acc"),
@@ -754,7 +764,6 @@
         acc = buf(i, "acc")
         near = own_half(i)
         if near is not None:
-            near.start()
             near.wait()
         arrived[i]["core"].wait_recv()
         if near is not None:
@@ -764,6 +773,7 @@
             add_blocks(
                 acc, lambda *p: p, split, lambda p, q, s: (p, c, q, s), (Y, Z, X), None
             )
+        prefetch_half(i + 1)
         for half, (at, width) in enumerate(parts(i)):
             cols = pl.ds(at, width)
             if half == 0:
@@ -902,24 +912,92 @@
         copy.start()
         copy.wait()
 
+    storing = []
+
+    def settle():
+        while storing:
+            storing.pop().wait()
+
     def keep_grad(n, at, grad):
         columns = grad.shape[1]
         r = made[n].shape[4]
         low = grad.astype(BF16).reshape(Y, 2, Z, X, r, columns)
-        stage[:, :, :, :, :, :columns] = low
-        fetch(stage.at[:, :, :, :, :, pl.ds(0, columns)], made[n].at[:, :, :, :, :, pl.ds(at, columns)])
-
-    def base_block(at, columns, first):
-        block = bstage.at[:, pl.ds(0, columns)]
+        settle()
+        gstage[:, :, :, :, :, :columns] = low
+        copy = pltpu.make_async_copy(
+            gstage.at[:, :, :, :, :, pl.ds(0, columns)],
+            made[n].at[:, :, :, :, :, pl.ds(at, columns)],
+            loads.at[0],
+        )
+        copy.start()
+        storing.append(copy)
+
+    all_base, all_value = column_blocks(w_base.shape[5]), column_blocks(w_value.shape[5])
+    weight_order = [(w_base,) + block for block in all_base[1:] + all_base[:1]]
+    weight_order += [(w_value,) + block for block in all_value]
+    coming = {}
+
+    def weight_copy(number):
+        full, at, columns = weight_order[number]
+        return pltpu.make_async_copy(
+            full.at[:, :, :, :, :, pl.ds(at, columns)],
+            stage.at[:, :, :, :, :, pl.ds(0, columns)],
+            loads.at[1],
+        )
+
+    def next_weight(number):
+        if number < len(weight_order):
+            coming["weight"] = weight_copy(number)
+            coming["weight"].start()
+
+    def rest_copy(number):
+        full, at, columns = weight_order[number]
+        if at == 0:
+            return pltpu.make_async_copy(
+                base_rest.at[:, pl.ds(0, columns - zw)],
+                bstage.at[:, pl.ds(zw, columns - zw)],
+                loads.at[2],
+            )
+        return pltpu.make_async_copy(
+            base_rest.at[:, pl.ds(at - zw, columns)], bstage.at[:, pl.ds(0, columns)], loads.at[2]
+        )
+
+    def next_rest(number):
+        if number < len(all_base):
+            coming["rest"] = rest_copy(number)
+            coming["rest"].start()
+
+    def next_pre(number):
+        if number < len(all_value):
+            at, columns = all_value[number]
+            coming["pre"] = pltpu.make_async_copy(
+                value_pre.at[:, pl.ds(at, columns)], pstage.at[:, pl.ds(0, columns)], loads.at[3]
+            )
+            coming["pre"].start()
+
+    def begin_fetch():
+        next_weight(0)
+        next_rest(0)
+        next_pre(0)
+        coming["x"] = pltpu.make_async_copy(pre, x_acc, loads.at[4])
+        coming["x"].start()
+        mixed_t[...] = mixed[...].astype(F32).T.astype(BF16)
+
+    def weight_here(columns):
+        coming["weight"].wait()
+        return stage[:, :, :, :, :, 0:columns].reshape(-1, columns)
+
+    def base_block(number):
+        full, at, columns = weight_order[number]
+        coming["rest"].wait()
         if at == 0:
             bstage[:, :zw] = zlow[...]
-            fetch(base_rest.at[:, pl.ds(0, columns - zw)], bstage.at[:, pl.ds(zw, columns - zw)])
-        else:
-            fetch(base_rest.at[:, pl.ds(at - zw, columns)], block)
-        low = block[...]
-        keep_grad(0, at, dot_t(mixed[...], low))
-        part = mm_t(low, weight_block(w_base, stage, load, at, columns))
-        mixed_acc[...] = part if first else mixed_acc[...] + part
+        low = bstage[:, :columns]
+        keep_grad(0, at, mm(mixed_t[...], low))
+        part = mm_t(low, weight_here(columns))
+        mixed_acc[...] = part if number == 0 else mixed_acc[...] + part
+        next_weight(number + 1)
+        next_rest(number + 1)
 
     def load_values(k):
         fetch(vals.at[k], vstage)
@@ -980,21 +1058,24 @@
         for copy in val_copies:
             copy.wait()
 
-    def value_block(at, columns, first):
+    def value_block(number):
+        full, at, columns = weight_order[len(all_base) + number]
         cols = pl.ds(at, columns)
+        if number == 0:
+            mixed_t[...] = x_low[...].reshape(rows, D).astype(F32).T.astype(BF16)
+            coming["x"].wait()
         grad = dot_t(probs[0], d_att[:, at : at + columns])
         for k in range(1, G):
             fetch(dvi.at[k - 1, :, cols], bstage.at[:, pl.ds(0, columns)])
             grad = grad + bstage[:, :columns].astype(F32)
-        fetch(value_pre.at[:, cols], pstage.at[:, pl.ds(0, columns)])
+        coming["pre"].wait()
         v = pstage[:, :columns]
         gate = jax.nn.sigmoid(v)
-        vlow[:, :columns] = (grad * (gate * (1.0 + v * (1.0 - gate)))).astype(BF16)
-        keep_grad(1, at, dot_t(x_low[...].reshape(rows, D), vlow[:, :columns]))
-        part = mm_t(vlow[:, :columns], weight_block(w_value, stage, load, at, columns))
-        if first:
-            fetch(pre, x_acc)
-        x_acc[...] += part
+        low = (grad * (gate * (1.0 + v * (1.0 - gate)))).astype(BF16)
+        next_pre(number + 1)
+        keep_grad(1, at, mm(mixed_t[...], low))
+        x_acc[...] += mm_t(low, weight_here(columns))
+        next_weight(len(all_base) + number + 1)
 
     def d_ema(t):
         v = ema[t]
@@ -1050,23 +1131,21 @@
     zs = [wire.to(y, c, (z + k) % Z, x) for k in range(1, Z)]
 
     run = functools.partial
-    base_blocks = column_blocks(w_base.shape[5])
-    value_blocks = column_blocks(w_value.shape[5])
-    todo = []
-    for number, block in enumerate(base_blocks[1:]):
-        todo.append((0, run(base_block, *block, number == 0), (n_base, block[0])))
+    todo = [(0, begin_fetch)]
+    for number in range(len(all_base) - 1):
+        todo.append((0, run(base_block, number), (n_base, weight_order[number][1])))
     for k in list(range(1, G))[::-1] + [0]:
         todo.append((0, run(load_values, k)))
         todo += [(0, run(scores_back, k, i)) for i in range(rows // QB)]
         todo.append((0, run(keys_back, k)))
         if k:
             todo.append((0, run(values_back, k)))
-    todo.append((0, run(base_block, *base_blocks[0], False), (n_base, 0)))
+    todo.append((0, run(base_block, len(all_base) - 1), (n_base, 0)))
     todo += [(0, run(d_ema, t)) for t in range(tiles)]
     todo += [(0, run(ends, t)) for t in range(tiles)]
     todo += [(0, exchange), (0, values_here)]
-    for number, block in enumerate(value_blocks):
-        todo.append((0, run(value_block, *block, number == 0), (n_value, block[0])))
+    for number, block in enumerate(all_value):
+        todo.append((0, run(value_block, number), (n_value, block[0])))
     todo.append((0, carries))
     todo += [(0, run(back, t)) for t in range(tiles)]
     todo += [(0, lambda: begin(1)), (0, tile_x), (0, buckets, "small")]
@@ -1081,10 +1160,10 @@
     for i in range(min(LEAD, total)):
         steps.append((run(stage_core, i), needs(i)))
     steps.append(lambda: begin(0))
-    for turn in range(total + 3 * LAG):
+    for turn in range(total + 3 * BLAG):
         for what, lag in ((stage_four, 3), (stage_three, 2), (stage_two, 1), (stage_one, 0)):
-            if 0 <= turn - lag * LAG < total:
-                steps.append(run(what, turn - lag * LAG))
+            if 0 <= turn - lag * BLAG < total:
+                steps.append(run(what, turn - lag * BLAG))
         if turn + LEAD < total:
             steps.append((run(stage_core, turn + LEAD), needs(turn + LEAD)))
         if turn >= total:
@@ -1101,6 +1180,7 @@
 
 LEAD = 3
 MOST = 1
+BLAG = 2
 
 
 def dot_t(a, b):
@@ -1178,7 +1258,6 @@
         pltpu.SemaphoreType.DMA((2,)),
         pltpu.VMEM((T, R, LANES), F32),
         pltpu.VMEM((T, R, LANES), F32),
-        pltpu.VMEM((T, R, LANES), F32),
         pltpu.VMEM((T, LANES, LANES), F32),
         pltpu.VMEM((D, LANES), F32),
         pltpu.VMEM((Y, 2, Z, X, share, LANES), F32),
@@ -1199,10 +1278,12 @@
         pltpu.VMEM((G - 1, R, zw), BF16),
         pltpu.VMEM((G - 1, R, zw), BF16),
         pltpu.VMEM((R, zw), BF16),
-        pltpu.VMEM((R, 768), BF16),
         pltpu.VMEM((R, D), F32),
         pltpu.VMEM((R, D), F32),
         pltpu.SemaphoreType.DMA,
+        pltpu.VMEM((Y, 2, Z, X, share, 768), BF16),
+        pltpu.VMEM((D, R), BF16),
+        pltpu.SemaphoreType.DMA((5,)),
     ]
     scratch += [pltpu.VMEM((2, Y, Z, X, r, widest[r]), BF16) for r in heights]
     order = (

time: 333 us -> 307 us (0.922)
  Pallas kernels: 264 us -> 239 us
    pallas_call x1, Pallas kernels: 147 us -> 121 us  [backward_all(): pl.pallas_call(body, out_shape=outs, in_specs=[ANY] * known + [spec for n...]
where the time goes in v1:
time: 307 us; the launch traced here: 302 us
  Pallas kernels  239 us (78%)
  matrix products  25.1 us (8%)
  local copies, waits for them, and re-layouts  20.4 us (7%)
  other arithmetic  16.3 us (5%)
    pallas_call x1, Pallas kernels, backward_all(): pl.pallas_call(body, out_shape=outs, in_specs=[ANY] * known + [spec for n...  121 us
    pallas_call x1, Pallas kernels, forward_all(): pl.pallas_call(body, out_shape=outs, in_specs=[ANY] * (2 + count) + [VM]...  117 us
    unnamed x64, local copies, waits for them, and re-layouts  12 us
    dot_general x3, matrix products, wgrad(): lax.dot_general(a, b, (((0,), (0,)), ((), ())), preferred_element_type=F32)  10.4 us
    dot_general x3, matrix products, mm(): return jnp.dot(a, b, preferred_element_type=F32)  7.46 us
    dot_general x3, matrix products, mm_t(): lax.dot_general(a, b, (((1,), (1,)), ((), ())), preferred_element_type=F32)  7.2 us

profile of v1, /device:TPU:0, one launch (start us, length us, event | category | flops | bytes accessed | tf_op | source)
XLA Modules:
  0.0 301.9 jit_solution(9127501946500456973)
XLA Ops:
  0.7 0.8 copy.68
  1.4 0.8 copy.69
  2.2 0.8 copy.70
  3.7 0.8 copy.71
  4.5 0.7 copy.72
  5.2 0.7 copy.73
  6.0 0.7 copy.74
  6.7 0.7 concatenate.12.refs_2_
  7.4 117.4 %forward_all.1 = (bf16[4,128,768]{2,1,0:T(8,128)(2,1)}, bf16[4,128,768]{2,1,0:T(8,128)(2,1)}, bf16[2,2,4,2,24,128]{5,4,3,2,1,0:T(8,128)(2,1)}, bf16[2,2,4,2,24,1...) custom-call(bf16[2,2,128,768]{3,2,1,0:T(8,128)(2,1)} %refs_0_.1, ...), custom_call_target="tpu_custom_call" | custom-call | tf_op jit(solution)/shard_map/forward_all/pallas_call | solution.py:649
  124.8 3.9 %multiply_convert_fusion.3 = bf16[512,1536]{1,0:T(8,128)(2,1)S(1)} fusion(f32[512,1536]{1,0:T(8,128)} %get-tuple-element.49, f32[512,3200]{1,0:T(8,128)} %get-tuple-element.48), kind=kLoop, calls=%fused_computation.10 | loop fusion | flops 4718592 | bytes 7864320 | tf_op jit(solution)/shard_map/convert_element_type | solution.py:1754
  128.7 0.8 copy-done.1
  129.7 3.9 %fusion.19 = (f32[512]{0:T(512)S(1)}, f32[512,768]{1,0:T(8,128)S(1)}, f32[512,768]{1,0:T(8,128)S(1)}) fusion(f32[512,3200]{1,0:T(8,128)S(1)} %copy-done.1, bf16[4,128,768]{2,1,0:T(8,128)(2,1)S(1)} %copy-done.3, bf16[512,1536]{1,0:T(8,128)(2,1)S(1)} %multiply_convert_fusion.3, bf16[1536,768]{1,0:T(8,128)(2,1)} %bitcast.83), kind=kOutput, calls=%fused_computation.81 | convolution fusion | flops 1213070848 | bytes 11012096 | tf_op jit(solution)/shard_map/dot_general | solution.py:1653
  133.9 0.8 slice_reduce_fusion.3
  134.8 1.5 fusion.18
  136.4 2.1 fusion.20
  138.9 0.8 copy-done
  139.7 1.6 fusion.8
  142.0 1.9 fusion.1
  143.9 1.8 multiply_reduce_fusion.1
  146.5 2.9 multiply_convert_fusion.5
  149.4 3.5 %multiply_reduce_fusion = (f32[512]{0:T(512)S(1)}, bf16[512,1536]{1,0:T(8,128)(2,1)}, bf16[512,1536]{1,0:T(8,128)(2,1)S(1)}) fusion(f32[512,1536]{1,0:T(8,128)S(1)} %copy-done.2, f32[512,3200]{1,0:T(8,128)S(1)} %copy-done.1, bf16[512,768]{1,0:T(8,128)(2,1)S(1)} %get-tuple-element.146, bf16[1536,768]{1,0:T(8,128)(2,1)S(1)} %bitcast.84), kind=kOutput, calls=%fused_computation.6 | convolution fusion | flops 1220541952 | bytes 12584960 | tf_op jit(solution)/shard_map/dot_general | solution.py:1657
  152.9 2.1 pad_maximum_fusion.refs_14_
  155.0 0.9 copy.75.refs_5_
  155.9 4.4 %convolution_convert_fusion = bf16[1536,768]{1,0:T(8,128)(2,1)} fusion(bf16[512,1536]{1,0:T(8,128)(2,1)} %copy-done.6, bf16[512,768]{1,0:T(8,128)(2,1)S(1)} %get-tuple-element.146), kind=kOutput, calls=%fused_computation | convolution fusion | flops 1209139200 | bytes 4718592 | tf_op jit(solution)/shard_map/dot_general | solution.py:1661
  160.3 3.1 %convolution_convert_fusion.1 = bf16[768,1536]{1,0:T(8,128)(2,1)} fusion(bf16[512,1536]{1,0:T(8,128)(2,1)S(1)} %copy-done.24, f32[512,768]{1,0:T(8,128)S(1)} %get-tuple-element.143, f32[768]{0:T(1024)S(1)} %bitcast.73, f32[512]{0:T(512)S(1)} %add_rsqrt_fusion.1, f32[512]{0:T(512)S(1)} %broadcast_multiply_fusion.4), kind=kOutput, calls=%fused_computation.1 | convolution fusion | flops 1210712064 | bytes 5512192 | tf_op jit(solution)/shard_map/dot_general | solution.py:1661
  163.4 2.9 convolution_convert_fusion.2
  166.3 1.7 slice.50.refs_10_
  168.6 121.4 %backward_all.1 = (f32[48,768]{1,0:T(8,128)}, f32[24,1536]{1,0:T(8,128)}, f32[48,768]{1,0:T(8,128)}, f32[24,3200]{1,0:T(8,128)}, f32[24,1536]{1,0:T(8,128)}, /*i...) custom-call(bf16[2,2,4,2,48,768]{5,4,3,2,1,0:T(8,128)(2,1)} %bitcast, ...), custom_call_target="tpu_custom_call" | custom-call | tf_op jit(solution)/shard_map/backward_all/pallas_call | solution.py:1308
  290.1 2.5 convert_element_type.104
  295.4 0.7 slice_reduce_fusion
  297.2 0.9 copy.90
  298.7 0.7 copy.92
  (81 shorter events, 10.5 us)
Async XLA Ops:
  124.8 4.7 %copy-start.1 = (f32[512,3200]{1,0:T(8,128)S(1)}, f32[512,3200]{1,0:T(8,128)}, u32[]{:S(2)}) copy-start(f32[512,3200]{1,0:T(8,128)} %get-tuple-element.48) | copy-start | bytes 19660804
  124.8 4.9 %copy-start.3 = (bf16[4,128,768]{2,1,0:T(8,128)(2,1)S(1)}, bf16[4,128,768]{2,1,0:T(8,128)(2,1)}, u32[]{:S(2)}) copy-start(bf16[4,128,768]{2,1,0:T(8,128)(2,1)} %get-tuple-element.47.refs_3_) | copy-start | bytes 2359300
  128.7 4.9 %copy-start.6 = (bf16[512,1536]{1,0:T(8,128)(2,1)}, bf16[512,1536]{1,0:T(8,128)(2,1)S(1)}, u32[]{:S(2)}) copy-start(bf16[512,1536]{1,0:T(8,128)(2,1)S(1)} %multiply_convert_fusion.3) | copy-start | bytes 4718596
  129.7 5.0 %copy-start.19 = (bf16[2,2,4,2,24,1536]{5,4,3,2,1,0:T(8,128)(2,1)S(1)}, bf16[2,2,4,2,24,1536]{5,4,3,2,1,0:T(8,128)(2,1)}, u32[]{:S(2)}) copy-start(bf16[2,2,4,2,24,1536]{5,4,3,2,1,0:T(8,128)(2,1)} %get-tuple-element.52) | copy-start | bytes 7077892
  134.8 1.7 copy-start.20
  136.3 5.7 %copy-start.21 = (f32[512,1536]{1,0:T(8,128)}, f32[512,1536]{1,0:T(8,128)S(1)}, u32[]{:S(2)}) copy-start(f32[512,1536]{1,0:T(8,128)S(1)} %fusion.18) | copy-start | bytes 9437188
  138.5 1.1 copy-start
  142.0 1.9 copy-start.4
  143.9 1.8 copy-start.23
  146.5 2.9 copy-start.2
  146.5 2.9 copy-start.18
  155.9 4.4 %copy-start.24 = (bf16[512,1536]{1,0:T(8,128)(2,1)S(1)}, bf16[512,1536]{1,0:T(8,128)(2,1)}, u32[]{:S(2)}) copy-start(bf16[512,1536]{1,0:T(8,128)(2,1)} %copy-done.23) | copy-start | bytes 4718596
  160.3 3.1 %copy-start.5 = (f32[512,768]{1,0:T(8,128)S(1)}, f32[512,768]{1,0:T(8,128)}, u32[]{:S(2)}) copy-start(f32[512,768]{1,0:T(8,128)} %copy-done.4) | copy-start | bytes 4718596
  160.3 3.1 %copy-start.22 = (f32[512,1536]{1,0:T(8,128)S(1)}, f32[512,1536]{1,0:T(8,128)}, u32[]{:S(2)}) copy-start(f32[512,1536]{1,0:T(8,128)} %copy-done.21) | copy-start | bytes 9437188
  163.4 4.6 %copy-start.15 = (f32[128]{0:T(128)S(1)}, f32[128]{0:T(128)}, u32[]{:S(2)}) copy-start(f32[128]{0:T(128)} %param.34) | copy-start | bytes 1540
  163.4 4.6 %copy-start.16 = (f32[128]{0:T(128)S(1)}, f32[128]{0:T(128)}, u32[]{:S(2)}) copy-start(f32[128]{0:T(128)} %param.36) | copy-start | bytes 1540
  290.0 2.6 copy-start.14
  290.0 2.6 copy-start.9
  290.0 6.1 %copy-start.17 = (f32[8,128]{1,0:T(8,128)S(1)}, f32[8,128]{1,0:T(8,128)}, u32[]{:S(2)}) copy-start(f32[8,128]{1,0:T(8,128)} %get-tuple-element.75) | copy-start | bytes 12292
  290.0 7.1 %copy-start.7 = (bf16[2,2,128,768]{3,2,1,0:T(8,128)(2,1)S(1)}, bf16[2,2,128,768]{3,2,1,0:T(8,128)(2,1)}, u32[]{:S(2)}) copy-start(bf16[2,2,128,768]{3,2,1,0:T(8,128)(2,1)} %get-tuple-element.180) | copy-start | bytes 2359300
  290.1 8.0 %copy-start.13 = (f32[24,1536]{1,0:T(8,128)S(1)}, f32[24,1536]{1,0:T(8,128)}, u32[]{:S(2)}) copy-start(f32[24,1536]{1,0:T(8,128)} %get-tuple-element.182) | copy-start | bytes 442372
  292.6 6.2 %copy-start.8 = (f32[24,3200]{1,0:T(8,128)S(1)}, f32[24,3200]{1,0:T(8,128)}, u32[]{:S(2)}) copy-start(f32[24,3200]{1,0:T(8,128)} %get-tuple-element.183) | copy-start | bytes 921604
  292.6 6.9 %copy-start.12 = (f32[48,768]{1,0:T(8,128)S(1)}, f32[48,768]{1,0:T(8,128)}, u32[]{:S(2)}) copy-start(f32[48,768]{1,0:T(8,128)} %get-tuple-element.184) | copy-start | bytes 442372
  292.6 7.6 %copy-start.11 = (f32[24,1536]{1,0:T(8,128)S(1)}, f32[24,1536]{1,0:T(8,128)}, u32[]{:S(2)}) copy-start(f32[24,1536]{1,0:T(8,128)} %get-tuple-element.185) | copy-start | bytes 442372
  294.7 6.0 %copy-start.10 = (f32[48,768]{1,0:T(8,128)S(1)}, f32[48,768]{1,0:T(8,128)}, u32[]{:S(2)}) copy-start(f32[48,768]{1,0:T(8,128)} %get-tuple-element.186) | copy-start | bytes 442372

commit v2 on v1

--- a/solution.py
+++ b/solution.py
@@ -96,8 +96,8 @@
 
 
 ALPHA = 0.5
-AHEAD = 2
-LAG = 2
+AHEAD = 3
+LAG = 3
 ORDER = 1
 LIMIT = 800
 
@@ -437,7 +437,7 @@
 
 
 def forward_kernel(lay, count, chunks, H, refs):
-    n_in, n_out = 2 + count, 15 + count
+    n_in, n_out = 2 + count, 16 + count
     ins = refs[:n_in]
     query_gain, query_bias, key_gain, relative = refs[n_in : n_in + 4]
     refs = refs[n_in + 4 :]
@@ -445,7 +445,7 @@
     tok_out, cot_out = outs[0], outs[1]
     fulls = outs[2 : 2 + count]
     mixed, ema, si, ri, table, turned = outs[2 + count : 8 + count]
-    value_pre, base, queries, keys, vals, probs, attended = outs[8 + count :]
+    value_pre, base, queries, keys, vals, probs, attended, z_out = outs[8 + count :]
     sems, work = scratch[:6], scratch[6:]
     xt, pack, raw, s_end, r_end, mine, inbox, inc, stage, strip, scores, load, c_send, c_recv = work
     wire, (begin, wait), stages, gathered, finish = gather_kernel(
@@ -483,6 +483,7 @@
 
     def send_keys():
         z_pre = base[:, :zw]
+        z_out[...] = z_pre
         shared = z_pre * jax.nn.sigmoid(z_pre)
         queries[...] = (shared * query_gain[...] + query_bias[...]).astype(BF16)
         keys[0] = (shared * key_gain[...]).astype(BF16)
@@ -641,6 +642,7 @@
         jax.ShapeDtypeStruct((G, R, V), BF16),
         jax.ShapeDtypeStruct((G, R, R), BF16),
         jax.ShapeDtypeStruct((R, V), F32),
+        jax.ShapeDtypeStruct((R, zw), F32),
     ]
 
     def body(*refs):
@@ -650,7 +652,7 @@
         body,
         out_shape=outs,
         in_specs=[ANY] * (2 + count) + [VM] * 3 + [SM],
-        out_specs=[VM] + [ANY] * (1 + count) + [VM] * 13,
+        out_specs=[VM] + [ANY] * (1 + count) + [VM] * 14,
         scratch_shapes=[
             pltpu.SemaphoreType.DMA((len(chunks) * per,)),
             pltpu.SemaphoreType.DMA((len(chunks) * per,)),
@@ -1711,30 +1713,28 @@
     def shift(value, k):
         return lax.ppermute(value, ("dp", "seq"), group_perm(k % G))
 
-    marks = jnp.broadcast_to(
-        stretch_size.reshape(1, -1).astype(BF16), (share, lay.MS)
-    )
+    marks = jnp.broadcast_to(stretch_size.reshape(-1, 1).astype(BF16), (lay.MS, share))
     used = 4 * H + 3 + lay.MS
     pack = jnp.concatenate(
         [
-            ema_delta,
-            ema_alpha,
-            ema_beta,
-            ema_gamma,
-            ema_omega[:, None],
-            first_gain[:, None],
-            second_gain[:, None],
+            ema_delta.T,
+            ema_alpha.T,
+            ema_beta.T,
+            ema_gamma.T,
+            ema_omega[None],
+            first_gain[None],
+            second_gain[None],
             marks,
-            jnp.zeros((share, LANES - used), BF16),
+            jnp.zeros((LANES - used, share), BF16),
         ],
-        1,
-    )
+        0,
+    ).T
     x_blocks, cot_blocks, fulls, rest = forward_all(
         lay, H, tokens, cotangent, (pack, w_value, w_base, w_out, w_up, w_down),
         query_gain[None], query_bias[None], key_gain[None], relative_bias,
     )
     mixed, ema_tiles, s_in, r_in, table, turned = rest[:6]
-    value_pre, base, queries, keys_all, vals_all, probs, attended = rest[6:]
+    value_pre, base, queries, keys_all, vals_all, probs, attended, z_pre = rest[6:]
     flags = jnp.stack([g_at, g_at])
     mats = [full.reshape(-1, full.shape[-1]) for full in fulls[1:]]
     mat_value, mat_base, mat_out, mat_up, mat_down = mats
@@ -1745,7 +1745,6 @@
     x = x_low.astype(F32)
     grad_out = cot_blocks.reshape(R, D).astype(F32)
 
-    z_pre = base[:, :zw]
     reset_pre = base[:, zw : zw + V]
     cand_pre = base[:, zw + V : zw + V + D]
     update_pre = base[:, zw + V + D :]
@@ -1808,12 +1807,12 @@
         ),
         share,
     )
-    own = reduced[5]
-    corr, lagged = own[:, :H], own[:, H : 2 * H]
-    p = jax.nn.sigmoid(ema_delta.astype(F32))
-    a = jax.nn.sigmoid(ema_alpha.astype(F32))
-    beta = ema_beta.astype(F32)
-    read = ema_gamma.astype(F32) * (H ** (-0.5))
+    own = reduced[5].T
+    corr, lagged = own[:H], own[H : 2 * H]
+    p = jax.nn.sigmoid(ema_delta.T.astype(F32))
+    a = jax.nn.sigmoid(ema_alpha.T.astype(F32))
+    beta = ema_beta.T.astype(F32)
+    read = ema_gamma.T.astype(F32) * (H ** (-0.5))
     q_grad = read * p * beta * lagged
     return (
         moved[0],
@@ -1823,13 +1822,13 @@
         reduced[2],
         reduced[1],
         reduced[0],
-        (read * beta * corr - a * q_grad) * p * (1.0 - p),
-        -p * q_grad * a * (1.0 - a),
-        p * read * corr,
-        p * beta * corr * (H ** (-0.5)),
-        own[:, 2 * H],
-        own[:, 2 * H + 1],
-        own[:, 2 * H + 2],
+        ((read * beta * corr - a * q_grad) * p * (1.0 - p)).T,
+        (-p * q_grad * a * (1.0 - a)).T,
+        (p * read * corr).T,
+        (p * beta * corr * (H ** (-0.5))).T,
+        own[2 * H],
+        own[2 * H + 1],
+        own[2 * H + 2],
         small_total[0, :zw],
         small_total[1, :zw],
         small_total[2, :zw],

time: 307 us -> 302 us (0.984)
  Pallas kernels: 239 us -> 235 us
    pallas_call x1, Pallas kernels: 117 us -> 112 us  [forward_all(): pl.pallas_call(body, out_shape=outs, in_specs=[ANY] * (2 + count) + [VM]...]
    unnamed x64 -> x62, local copies, waits for them, and re-layouts: 12 us -> 12.1 us
where the time goes in v2:
time: 302 us; the launch traced here: 297 us
  Pallas kernels  235 us (78%)
  matrix products  25.2 us (8%)
  local copies, waits for them, and re-layouts  18.7 us (6%)
  other arithmetic  16.3 us (5%)
    pallas_call x1, Pallas kernels, backward_all(): pl.pallas_call(body, out_shape=outs, in_specs=[ANY] * known + [spec for n...  123 us
    pallas_call x1, Pallas kernels, forward_all(): pl.pallas_call(body, out_shape=outs, in_specs=[ANY] * (2 + count) + [VM]...  112 us
    unnamed x62, local copies, waits for them, and re-layouts  12.1 us
    dot_general x3, matrix products, wgrad(): lax.dot_general(a, b, (((0,), (0,)), ((), ())), preferred_element_type=F32)  10.5 us
    dot_general x3, matrix products, mm(): return jnp.dot(a, b, preferred_element_type=F32)  7.46 us
    dot_general x3, matrix products, mm_t(): lax.dot_general(a, b, (((1,), (1,)), ((), ())), preferred_element_type=F32)  7.22 us

profile of v2, /device:TPU:0, one launch (start us, length us, event | category | flops | bytes accessed | tf_op | source)
XLA Modules:
  0.0 297.0 jit_solution(4578206239585715396)
XLA Ops:
  0.7 0.8 copy.48
  1.4 0.8 copy.49
  2.2 0.8 copy.50
  3.0 0.8 copy.51
  3.7 0.7 convert_element_type.83
  4.5 0.7 copy.52
  5.2 0.7 copy.53
  6.0 0.7 copy.54
  6.7 0.7 concatenate.12
  7.4 112.4 %forward_all.1 = (bf16[4,128,768]{2,1,0:T(8,128)(2,1)}, bf16[4,128,768]{2,1,0:T(8,128)(2,1)}, bf16[2,2,4,2,24,128]{5,4,3,2,1,0:T(8,128)(2,1)}, bf16[2,2,4,2,24,1...) custom-call(bf16[2,2,128,768]{3,2,1,0:T(8,128)(2,1)} %refs_0_.1, ...), custom_call_target="tpu_custom_call" | custom-call | tf_op jit(solution)/shard_map/forward_all/pallas_call | solution.py:651
  119.8 3.9 %multiply_convert_fusion.3 = bf16[512,1536]{1,0:T(8,128)(2,1)S(1)} fusion(f32[512,1536]{1,0:T(8,128)} %get-tuple-element.50, f32[512,3200]{1,0:T(8,128)} %get-tuple-element.49), kind=kLoop, calls=%fused_computation.10 | loop fusion | flops 4718592 | bytes 7864320 | tf_op jit(solution)/shard_map/convert_element_type | solution.py:1753
  123.7 0.8 copy-done.1
  124.7 3.9 %fusion.22 = (f32[512]{0:T(512)S(1)}, f32[512,768]{1,0:T(8,128)S(1)}, f32[512,768]{1,0:T(8,128)S(1)}) fusion(f32[512,3200]{1,0:T(8,128)S(1)} %copy-done.1, bf16[4,128,768]{2,1,0:T(8,128)(2,1)S(1)} %copy-done.3, bf16[512,1536]{1,0:T(8,128)(2,1)S(1)} %multiply_convert_fusion.3, bf16[1536,768]{1,0:T(8,128)(2,1)} %bitcast.121), kind=kOutput, calls=%fused_computation.84 | convolution fusion | flops 1213070848 | bytes 11012096 | tf_op jit(solution)/shard_map/dot_general | solution.py:1655
  128.9 0.8 slice_reduce_fusion.3
  129.8 1.5 fusion.21
  131.4 2.1 fusion.23
  133.8 0.8 copy-done
  134.7 1.6 fusion.8
  137.0 1.9 fusion.1
  138.9 1.8 multiply_reduce_fusion.1
  141.5 2.8 multiply_convert_fusion.5
  144.4 3.6 %multiply_reduce_fusion = (f32[512]{0:T(512)S(1)}, bf16[512,1536]{1,0:T(8,128)(2,1)}, bf16[512,1536]{1,0:T(8,128)(2,1)S(1)}) fusion(f32[512,1536]{1,0:T(8,128)S(1)} %copy-done.2, f32[512,3200]{1,0:T(8,128)S(1)} %copy-done.1, bf16[512,768]{1,0:T(8,128)(2,1)S(1)} %get-tuple-element.130, bf16[1536,768]{1,0:T(8,128)(2,1)S(1)} %bitcast.122), kind=kOutput, calls=%fused_computation.6 | convolution fusion | flops 1220541952 | bytes 12584960 | tf_op jit(solution)/shard_map/dot_general | solution.py:1659
  147.9 2.1 pad_maximum_fusion.refs_14_
  150.0 0.9 copy.55.refs_5_
  150.9 4.4 %convolution_convert_fusion = bf16[1536,768]{1,0:T(8,128)(2,1)} fusion(bf16[512,1536]{1,0:T(8,128)(2,1)} %copy-done.6, bf16[512,768]{1,0:T(8,128)(2,1)S(1)} %get-tuple-element.130), kind=kOutput, calls=%fused_computation | convolution fusion | flops 1209139200 | bytes 4718592 | tf_op jit(solution)/shard_map/dot_general | solution.py:1663
  155.3 3.1 %convolution_convert_fusion.1 = bf16[768,1536]{1,0:T(8,128)(2,1)} fusion(bf16[512,1536]{1,0:T(8,128)(2,1)S(1)} %copy-done.23, f32[512,768]{1,0:T(8,128)S(1)} %get-tuple-element.127, f32[768]{0:T(1024)S(1)} %bitcast.111, f32[512]{0:T(512)S(1)} %add_rsqrt_fusion.1, f32[512]{0:T(512)S(1)} %broadcast_multiply_fusion.4), kind=kOutput, calls=%fused_computation.1 | convolution fusion | flops 1210712064 | bytes 5512192 | tf_op jit(solution)/shard_map/dot_general | solution.py:1663
  158.4 3.0 %convolution_convert_fusion.2 = bf16[1536,768]{1,0:T(8,128)(2,1)} fusion(f32[512,768]{1,0:T(8,128)S(1)} %copy-done.5, f32[512,1536]{1,0:T(8,128)S(1)} %copy-done.21), kind=kOutput, calls=%fused_computation.2 | convolution fusion | flops 1213464576 | bytes 7077888 | tf_op jit(solution)/shard_map/dot_general | solution.py:1663
  162.1 123.1 %backward_all.1 = (f32[48,768]{1,0:T(8,128)}, f32[24,1536]{1,0:T(8,128)}, f32[48,768]{1,0:T(8,128)}, f32[24,3200]{1,0:T(8,128)}, f32[24,1536]{1,0:T(8,128)}, /*i...) custom-call(bf16[2,2,4,2,48,768]{5,4,3,2,1,0:T(8,128)(2,1)} %bitcast, ...), custom_call_target="tpu_custom_call" | custom-call | tf_op jit(solution)/shard_map/backward_all/pallas_call | solution.py:1310
  285.2 2.5 convert_element_type.104
  290.4 0.7 slice_reduce_fusion
  292.2 0.9 copy.66
  293.7 0.7 copy.68
  (77 shorter events, 9.8 us)
Async XLA Ops:
  119.8 4.7 %copy-start.1 = (f32[512,3200]{1,0:T(8,128)S(1)}, f32[512,3200]{1,0:T(8,128)}, u32[]{:S(2)}) copy-start(f32[512,3200]{1,0:T(8,128)} %get-tuple-element.49) | copy-start | bytes 19660804
  119.8 4.9 %copy-start.3 = (bf16[4,128,768]{2,1,0:T(8,128)(2,1)S(1)}, bf16[4,128,768]{2,1,0:T(8,128)(2,1)}, u32[]{:S(2)}) copy-start(bf16[4,128,768]{2,1,0:T(8,128)(2,1)} %get-tuple-element.48.refs_3_) | copy-start | bytes 2359300
  123.7 4.9 %copy-start.6 = (bf16[512,1536]{1,0:T(8,128)(2,1)}, bf16[512,1536]{1,0:T(8,128)(2,1)S(1)}, u32[]{:S(2)}) copy-start(bf16[512,1536]{1,0:T(8,128)(2,1)S(1)} %multiply_convert_fusion.3) | copy-start | bytes 4718596
  124.7 5.0 %copy-start.18 = (bf16[2,2,4,2,24,1536]{5,4,3,2,1,0:T(8,128)(2,1)S(1)}, bf16[2,2,4,2,24,1536]{5,4,3,2,1,0:T(8,128)(2,1)}, u32[]{:S(2)}) copy-start(bf16[2,2,4,2,24,1536]{5,4,3,2,1,0:T(8,128)(2,1)} %get-tuple-element.53) | copy-start | bytes 7077892
  129.8 1.7 copy-start.19
  131.3 5.7 %copy-start.20 = (f32[512,1536]{1,0:T(8,128)}, f32[512,1536]{1,0:T(8,128)S(1)}, u32[]{:S(2)}) copy-start(f32[512,1536]{1,0:T(8,128)S(1)} %fusion.21) | copy-start | bytes 9437188
  133.5 1.1 copy-start
  137.0 1.9 copy-start.4
  138.9 1.8 copy-start.22
  141.5 2.8 copy-start.2
  141.5 2.9 copy-start.17
  150.9 4.4 %copy-start.23 = (bf16[512,1536]{1,0:T(8,128)(2,1)S(1)}, bf16[512,1536]{1,0:T(8,128)(2,1)}, u32[]{:S(2)}) copy-start(bf16[512,1536]{1,0:T(8,128)(2,1)} %copy-done.22) | copy-start | bytes 4718596
  155.3 3.1 %copy-start.5 = (f32[512,768]{1,0:T(8,128)S(1)}, f32[512,768]{1,0:T(8,128)}, u32[]{:S(2)}) copy-start(f32[512,768]{1,0:T(8,128)} %copy-done.4) | copy-start | bytes 4718596
  155.3 3.1 %copy-start.21 = (f32[512,1536]{1,0:T(8,128)S(1)}, f32[512,1536]{1,0:T(8,128)}, u32[]{:S(2)}) copy-start(f32[512,1536]{1,0:T(8,128)} %copy-done.20) | copy-start | bytes 9437188
  158.4 3.0 %copy-start.14 = (f32[128]{0:T(128)S(1)}, f32[128]{0:T(128)}, u32[]{:S(2)}) copy-start(f32[128]{0:T(128)} %param.34) | copy-start | bytes 1540
  158.4 3.0 %copy-start.15 = (f32[128]{0:T(128)S(1)}, f32[128]{0:T(128)}, u32[]{:S(2)}) copy-start(f32[128]{0:T(128)} %param.36) | copy-start | bytes 1540
  285.1 2.5 copy-start.9
  285.1 6.0 %copy-start.16 = (f32[8,128]{1,0:T(8,128)S(1)}, f32[8,128]{1,0:T(8,128)}, u32[]{:S(2)}) copy-start(f32[8,128]{1,0:T(8,128)} %get-tuple-element.77) | copy-start | bytes 12292
  285.1 7.1 %copy-start.7 = (bf16[2,2,128,768]{3,2,1,0:T(8,128)(2,1)S(1)}, bf16[2,2,128,768]{3,2,1,0:T(8,128)(2,1)}, u32[]{:S(2)}) copy-start(bf16[2,2,128,768]{3,2,1,0:T(8,128)(2,1)} %get-tuple-element.164) | copy-start | bytes 2359300
  285.2 7.9 %copy-start.13 = (f32[24,1536]{1,0:T(8,128)S(1)}, f32[24,1536]{1,0:T(8,128)}, u32[]{:S(2)}) copy-start(f32[24,1536]{1,0:T(8,128)} %get-tuple-element.166) | copy-start | bytes 442372
  287.7 6.1 %copy-start.8 = (f32[24,3200]{1,0:T(8,128)S(1)}, f32[24,3200]{1,0:T(8,128)}, u32[]{:S(2)}) copy-start(f32[24,3200]{1,0:T(8,128)} %get-tuple-element.167) | copy-start | bytes 921604
  287.7 6.8 %copy-start.12 = (f32[48,768]{1,0:T(8,128)S(1)}, f32[48,768]{1,0:T(8,128)}, u32[]{:S(2)}) copy-start(f32[48,768]{1,0:T(8,128)} %get-tuple-element.168) | copy-start | bytes 442372
  287.7 7.5 %copy-start.11 = (f32[24,1536]{1,0:T(8,128)S(1)}, f32[24,1536]{1,0:T(8,128)}, u32[]{:S(2)}) copy-start(f32[24,1536]{1,0:T(8,128)} %get-tuple-element.169) | copy-start | bytes 442372
  289.8 6.0 %copy-start.10 = (f32[48,768]{1,0:T(8,128)S(1)}, f32[48,768]{1,0:T(8,128)}, u32[]{:S(2)}) copy-start(f32[48,768]{1,0:T(8,128)} %get-tuple-element.170) | copy-start | bytes 442372

commit v3 on v2

--- a/solution.py
+++ b/solution.py
@@ -1180,9 +1180,9 @@
     wire.finish()
 
 
-LEAD = 3
+LEAD = 2
 MOST = 1
-BLAG = 2
+BLAG = 3
 
 
 def dot_t(a, b):

time: 302 us -> 300 us (level)
  no operation moved by 1% of the time
where the time goes in v3:
time: 300 us; the launch traced here: 295 us
  Pallas kernels  233 us (78%)
  matrix products  25.2 us (8%)
  local copies, waits for them, and re-layouts  18.7 us (6%)
  other arithmetic  16.3 us (5%)
    pallas_call x1, Pallas kernels, backward_all(): pl.pallas_call(body, out_shape=outs, in_specs=[ANY] * known + [spec for n...  121 us
    pallas_call x1, Pallas kernels, forward_all(): pl.pallas_call(body, out_shape=outs, in_specs=[ANY] * (2 + count) + [VM]...  112 us
    unnamed x62, local copies, waits for them, and re-layouts  12.1 us
    dot_general x3, matrix products, wgrad(): lax.dot_general(a, b, (((0,), (0,)), ((), ())), preferred_element_type=F32)  10.5 us
    dot_general x3, matrix products, mm(): return jnp.dot(a, b, preferred_element_type=F32)  7.46 us
    dot_general x3, matrix products, mm_t(): lax.dot_general(a, b, (((1,), (1,)), ((), ())), preferred_element_type=F32)  7.22 us

profile of v3, /device:TPU:0, one launch (start us, length us, event | category | flops | bytes accessed | tf_op | source)
XLA Modules:
  0.0 294.8 jit_solution(5369351295176549224)
XLA Ops:
  0.7 0.8 copy.48
  1.4 0.8 copy.49
  2.2 0.8 copy.50
  3.0 0.8 copy.51
  3.7 0.7 convert_element_type.83
  4.5 0.7 copy.52
  5.2 0.7 copy.53
  6.0 0.7 copy.54
  6.7 0.7 concatenate.12
  7.4 112.4 %forward_all.1 = (bf16[4,128,768]{2,1,0:T(8,128)(2,1)}, bf16[4,128,768]{2,1,0:T(8,128)(2,1)}, bf16[2,2,4,2,24,128]{5,4,3,2,1,0:T(8,128)(2,1)}, bf16[2,2,4,2,24,1...) custom-call(bf16[2,2,128,768]{3,2,1,0:T(8,128)(2,1)} %refs_0_.1, ...), custom_call_target="tpu_custom_call" | custom-call | tf_op jit(solution)/shard_map/forward_all/pallas_call | solution.py:651
  119.8 3.9 %multiply_convert_fusion.3 = bf16[512,1536]{1,0:T(8,128)(2,1)S(1)} fusion(f32[512,1536]{1,0:T(8,128)} %get-tuple-element.50, f32[512,3200]{1,0:T(8,128)} %get-tuple-element.49), kind=kLoop, calls=%fused_computation.10 | loop fusion | flops 4718592 | bytes 7864320 | tf_op jit(solution)/shard_map/convert_element_type | solution.py:1753
  123.7 0.8 copy-done.1
  124.7 3.9 %fusion.22 = (f32[512]{0:T(512)S(1)}, f32[512,768]{1,0:T(8,128)S(1)}, f32[512,768]{1,0:T(8,128)S(1)}) fusion(f32[512,3200]{1,0:T(8,128)S(1)} %copy-done.1, bf16[4,128,768]{2,1,0:T(8,128)(2,1)S(1)} %copy-done.3, bf16[512,1536]{1,0:T(8,128)(2,1)S(1)} %multiply_convert_fusion.3, bf16[1536,768]{1,0:T(8,128)(2,1)} %bitcast.121), kind=kOutput, calls=%fused_computation.84 | convolution fusion | flops 1213070848 | bytes 11012096 | tf_op jit(solution)/shard_map/dot_general | solution.py:1655
  128.9 0.8 slice_reduce_fusion.3
  129.8 1.5 fusion.21
  131.4 2.1 fusion.23
  133.8 0.8 copy-done
  134.7 1.6 fusion.8
  137.0 1.9 fusion.1
  138.9 1.8 multiply_reduce_fusion.1
  141.5 2.8 multiply_convert_fusion.5
  144.4 3.6 %multiply_reduce_fusion = (f32[512]{0:T(512)S(1)}, bf16[512,1536]{1,0:T(8,128)(2,1)}, bf16[512,1536]{1,0:T(8,128)(2,1)S(1)}) fusion(f32[512,1536]{1,0:T(8,128)S(1)} %copy-done.2, f32[512,3200]{1,0:T(8,128)S(1)} %copy-done.1, bf16[512,768]{1,0:T(8,128)(2,1)S(1)} %get-tuple-element.130, bf16[1536,768]{1,0:T(8,128)(2,1)S(1)} %bitcast.122), kind=kOutput, calls=%fused_computation.6 | convolution fusion | flops 1220541952 | bytes 12584960 | tf_op jit(solution)/shard_map/dot_general | solution.py:1659
  147.9 2.1 pad_maximum_fusion.refs_14_
  150.0 0.9 copy.55.refs_5_
  150.9 4.4 %convolution_convert_fusion = bf16[1536,768]{1,0:T(8,128)(2,1)} fusion(bf16[512,1536]{1,0:T(8,128)(2,1)} %copy-done.6, bf16[512,768]{1,0:T(8,128)(2,1)S(1)} %get-tuple-element.130), kind=kOutput, calls=%fused_computation | convolution fusion | flops 1209139200 | bytes 4718592 | tf_op jit(solution)/shard_map/dot_general | solution.py:1663
  155.3 3.1 %convolution_convert_fusion.1 = bf16[768,1536]{1,0:T(8,128)(2,1)} fusion(bf16[512,1536]{1,0:T(8,128)(2,1)S(1)} %copy-done.23, f32[512,768]{1,0:T(8,128)S(1)} %get-tuple-element.127, f32[768]{0:T(1024)S(1)} %bitcast.111, f32[512]{0:T(512)S(1)} %add_rsqrt_fusion.1, f32[512]{0:T(512)S(1)} %broadcast_multiply_fusion.4), kind=kOutput, calls=%fused_computation.1 | convolution fusion | flops 1210712064 | bytes 5512192 | tf_op jit(solution)/shard_map/dot_general | solution.py:1663
  158.4 3.0 %convolution_convert_fusion.2 = bf16[1536,768]{1,0:T(8,128)(2,1)} fusion(f32[512,768]{1,0:T(8,128)S(1)} %copy-done.5, f32[512,1536]{1,0:T(8,128)S(1)} %copy-done.21), kind=kOutput, calls=%fused_computation.2 | convolution fusion | flops 1213464576 | bytes 7077888 | tf_op jit(solution)/shard_map/dot_general | solution.py:1663
  162.1 120.9 %backward_all.1 = (f32[48,768]{1,0:T(8,128)}, f32[24,1536]{1,0:T(8,128)}, f32[48,768]{1,0:T(8,128)}, f32[24,3200]{1,0:T(8,128)}, f32[24,1536]{1,0:T(8,128)}, /*i...) custom-call(bf16[2,2,4,2,48,768]{5,4,3,2,1,0:T(8,128)(2,1)} %bitcast, ...), custom_call_target="tpu_custom_call" | custom-call | tf_op jit(solution)/shard_map/backward_all/pallas_call | solution.py:1310
  283.0 2.5 convert_element_type.104
  288.3 0.7 slice_reduce_fusion
  290.1 0.9 copy.66
  291.6 0.7 copy.68
  (77 shorter events, 9.8 us)
Async XLA Ops:
  119.8 4.7 %copy-start.1 = (f32[512,3200]{1,0:T(8,128)S(1)}, f32[512,3200]{1,0:T(8,128)}, u32[]{:S(2)}) copy-start(f32[512,3200]{1,0:T(8,128)} %get-tuple-element.49) | copy-start | bytes 19660804
  119.8 4.9 %copy-start.3 = (bf16[4,128,768]{2,1,0:T(8,128)(2,1)S(1)}, bf16[4,128,768]{2,1,0:T(8,128)(2,1)}, u32[]{:S(2)}) copy-start(bf16[4,128,768]{2,1,0:T(8,128)(2,1)} %get-tuple-element.48.refs_3_) | copy-start | bytes 2359300
  123.7 4.9 %copy-start.6 = (bf16[512,1536]{1,0:T(8,128)(2,1)}, bf16[512,1536]{1,0:T(8,128)(2,1)S(1)}, u32[]{:S(2)}) copy-start(bf16[512,1536]{1,0:T(8,128)(2,1)S(1)} %multiply_convert_fusion.3) | copy-start | bytes 4718596
  124.7 5.0 %copy-start.18 = (bf16[2,2,4,2,24,1536]{5,4,3,2,1,0:T(8,128)(2,1)S(1)}, bf16[2,2,4,2,24,1536]{5,4,3,2,1,0:T(8,128)(2,1)}, u32[]{:S(2)}) copy-start(bf16[2,2,4,2,24,1536]{5,4,3,2,1,0:T(8,128)(2,1)} %get-tuple-element.53) | copy-start | bytes 7077892
  129.8 1.7 copy-start.19
  131.3 5.7 %copy-start.20 = (f32[512,1536]{1,0:T(8,128)}, f32[512,1536]{1,0:T(8,128)S(1)}, u32[]{:S(2)}) copy-start(f32[512,1536]{1,0:T(8,128)S(1)} %fusion.21) | copy-start | bytes 9437188
  133.5 1.1 copy-start
  137.0 1.9 copy-start.4
  138.9 1.8 copy-start.22
  141.5 2.8 copy-start.2
  141.5 2.9 copy-start.17
  150.9 4.4 %copy-start.23 = (bf16[512,1536]{1,0:T(8,128)(2,1)S(1)}, bf16[512,1536]{1,0:T(8,128)(2,1)}, u32[]{:S(2)}) copy-start(bf16[512,1536]{1,0:T(8,128)(2,1)} %copy-done.22) | copy-start | bytes 4718596
  155.3 3.1 %copy-start.5 = (f32[512,768]{1,0:T(8,128)S(1)}, f32[512,768]{1,0:T(8,128)}, u32[]{:S(2)}) copy-start(f32[512,768]{1,0:T(8,128)} %copy-done.4) | copy-start | bytes 4718596
  155.3 3.1 %copy-start.21 = (f32[512,1536]{1,0:T(8,128)S(1)}, f32[512,1536]{1,0:T(8,128)}, u32[]{:S(2)}) copy-start(f32[512,1536]{1,0:T(8,128)} %copy-done.20) | copy-start | bytes 9437188
  158.4 3.0 %copy-start.14 = (f32[128]{0:T(128)S(1)}, f32[128]{0:T(128)}, u32[]{:S(2)}) copy-start(f32[128]{0:T(128)} %param.34) | copy-start | bytes 1540
  158.4 3.0 %copy-start.15 = (f32[128]{0:T(128)S(1)}, f32[128]{0:T(128)}, u32[]{:S(2)}) copy-start(f32[128]{0:T(128)} %param.36) | copy-start | bytes 1540
  283.0 2.5 copy-start.9
  283.0 6.0 %copy-start.16 = (f32[8,128]{1,0:T(8,128)S(1)}, f32[8,128]{1,0:T(8,128)}, u32[]{:S(2)}) copy-start(f32[8,128]{1,0:T(8,128)} %get-tuple-element.77) | copy-start | bytes 12292
  283.0 7.1 %copy-start.7 = (bf16[2,2,128,768]{3,2,1,0:T(8,128)(2,1)S(1)}, bf16[2,2,128,768]{3,2,1,0:T(8,128)(2,1)}, u32[]{:S(2)}) copy-start(bf16[2,2,128,768]{3,2,1,0:T(8,128)(2,1)} %get-tuple-element.164) | copy-start | bytes 2359300
  283.0 7.9 %copy-start.13 = (f32[24,1536]{1,0:T(8,128)S(1)}, f32[24,1536]{1,0:T(8,128)}, u32[]{:S(2)}) copy-start(f32[24,1536]{1,0:T(8,128)} %get-tuple-element.166) | copy-start | bytes 442372
  285.5 6.1 %copy-start.8 = (f32[24,3200]{1,0:T(8,128)S(1)}, f32[24,3200]{1,0:T(8,128)}, u32[]{:S(2)}) copy-start(f32[24,3200]{1,0:T(8,128)} %get-tuple-element.167) | copy-start | bytes 921604
  285.5 6.8 %copy-start.12 = (f32[48,768]{1,0:T(8,128)S(1)}, f32[48,768]{1,0:T(8,128)}, u32[]{:S(2)}) copy-start(f32[48,768]{1,0:T(8,128)} %get-tuple-element.168) | copy-start | bytes 442372
  285.5 7.5 %copy-start.11 = (f32[24,1536]{1,0:T(8,128)S(1)}, f32[24,1536]{1,0:T(8,128)}, u32[]{:S(2)}) copy-start(f32[24,1536]{1,0:T(8,128)} %get-tuple-element.169) | copy-start | bytes 442372
  287.6 6.0 %copy-start.10 = (f32[48,768]{1,0:T(8,128)S(1)}, f32[48,768]{1,0:T(8,128)}, u32[]{:S(2)}) copy-start(f32[48,768]{1,0:T(8,128)} %get-tuple-element.170) | copy-start | bytes 442372

commit v4 on v3

--- a/solution.py
+++ b/solution.py
@@ -873,18 +873,22 @@
 
     small_at = [0]
 
-    def small_stage(moves):
-        copies = []
+    small_open = []
+
+    def small_begin(moves):
         for target in moves:
             slot = small_at[0]
             small_at[0] += 1
-            copies.append((slot, wire.start(small_acc, small_recv.at[slot], target)))
-        for slot, copy in copies:
+            small_open.append((slot, wire.start(small_acc, small_recv.at[slot], target)))
+
+    def small_end():
+        for slot, copy in small_open:
             copy.wait_send()
             wire.sent = [other for other in wire.sent if other is not copy]
-        for slot, copy in copies:
+        for slot, copy in small_open:
             copy.wait_recv()
             small_acc[...] += small_recv[slot]
+        small_open.clear()
 
     rows, tiles = xt.shape[1], xt.shape[0]
     per_block = rows // lay.BL
@@ -1142,6 +1146,7 @@
         todo.append((0, run(keys_back, k)))
         if k:
             todo.append((0, run(values_back, k)))
+    todo.append((0, buckets, "small"))
     todo.append((0, run(base_block, len(all_base) - 1), (n_base, 0)))
     todo += [(0, run(d_ema, t)) for t in range(tiles)]
     todo += [(0, run(ends, t)) for t in range(tiles)]
@@ -1150,7 +1155,7 @@
         todo.append((0, run(value_block, number), (n_value, block[0])))
     todo.append((0, carries))
     todo += [(0, run(back, t)) for t in range(tiles)]
-    todo += [(0, lambda: begin(1)), (0, tile_x), (0, buckets, "small")]
+    todo += [(0, lambda: begin(1)), (0, tile_x)]
     todo += [(0, run(correlate, t)) for t in range(tiles)]
     todo.append((0, share_sums, (len(grads) - 1, 0)))
 
@@ -1168,11 +1173,12 @@
                 steps.append(run(what, turn - lag * BLAG))
         if turn + LEAD < total:
             steps.append((run(stage_core, turn + LEAD), needs(turn + LEAD)))
-        if turn >= total:
-            late = turn - total
-            moves = ([wire.to(y, 1 - c, z, x)], xs, ys, zs)
-            if late < 4:
-                steps.append((run(small_stage, moves[late]), "small"))
+        hop = turn - (total - 4)
+        moves = ([wire.to(y, 1 - c, z, x)], xs, ys, zs)
+        if 1 <= hop <= len(moves):
+            steps.append(small_end)
+        if 0 <= hop < len(moves):
+            steps.append((run(small_begin, moves[hop]), "small"))
     interleave(steps, todo, MOST)
     small_out[...] = small_acc[...]
     wait(0)

time: 300 us -> 298 us (level)
  no operation moved by 1% of the time
where the time goes in v4:
time: 298 us; the launch traced here: 292 us
  Pallas kernels  231 us (78%)
  matrix products  25.2 us (8%)
  local copies, waits for them, and re-layouts  18.7 us (6%)
  other arithmetic  16.3 us (5%)
    pallas_call x1, Pallas kernels, backward_all(): pl.pallas_call(body, out_shape=outs, in_specs=[ANY] * known + [spec for n...  118 us
    pallas_call x1, Pallas kernels, forward_all(): pl.pallas_call(body, out_shape=outs, in_specs=[ANY] * (2 + count) + [VM]...  112 us
    unnamed x62, local copies, waits for them, and re-layouts  12.1 us
    dot_general x3, matrix products, wgrad(): lax.dot_general(a, b, (((0,), (0,)), ((), ())), preferred_element_type=F32)  10.5 us
    dot_general x3, matrix products, mm(): return jnp.dot(a, b, preferred_element_type=F32)  7.46 us
    dot_general x3, matrix products, mm_t(): lax.dot_general(a, b, (((1,), (1,)), ((), ())), preferred_element_type=F32)  7.22 us

profile of v4, /device:TPU:0, one launch (start us, length us, event | category | flops | bytes accessed | tf_op | source)
XLA Modules:
  0.0 292.1 jit_solution(12537358525322937840)
XLA Ops:
  0.7 0.8 copy.48
  1.4 0.8 copy.49
  2.2 0.8 copy.50
  3.0 0.8 copy.51
  3.7 0.7 convert_element_type.83
  4.5 0.7 copy.52
  5.2 0.7 copy.53
  6.0 0.7 copy.54
  6.7 0.7 concatenate.12
  7.4 112.4 %forward_all.1 = (bf16[4,128,768]{2,1,0:T(8,128)(2,1)}, bf16[4,128,768]{2,1,0:T(8,128)(2,1)}, bf16[2,2,4,2,24,128]{5,4,3,2,1,0:T(8,128)(2,1)}, bf16[2,2,4,2,24,1...) custom-call(bf16[2,2,128,768]{3,2,1,0:T(8,128)(2,1)} %refs_0_.1, ...), custom_call_target="tpu_custom_call" | custom-call | tf_op jit(solution)/shard_map/forward_all/pallas_call | solution.py:651
  119.8 3.9 %multiply_convert_fusion.3 = bf16[512,1536]{1,0:T(8,128)(2,1)S(1)} fusion(f32[512,1536]{1,0:T(8,128)} %get-tuple-element.50, f32[512,3200]{1,0:T(8,128)} %get-tuple-element.49), kind=kLoop, calls=%fused_computation.10 | loop fusion | flops 4718592 | bytes 7864320 | tf_op jit(solution)/shard_map/convert_element_type | solution.py:1759
  123.7 0.8 copy-done.1
  124.7 3.9 %fusion.22 = (f32[512]{0:T(512)S(1)}, f32[512,768]{1,0:T(8,128)S(1)}, f32[512,768]{1,0:T(8,128)S(1)}) fusion(f32[512,3200]{1,0:T(8,128)S(1)} %copy-done.1, bf16[4,128,768]{2,1,0:T(8,128)(2,1)S(1)} %copy-done.3, bf16[512,1536]{1,0:T(8,128)(2,1)S(1)} %multiply_convert_fusion.3, bf16[1536,768]{1,0:T(8,128)(2,1)} %bitcast.121), kind=kOutput, calls=%fused_computation.84 | convolution fusion | flops 1213070848 | bytes 11012096 | tf_op jit(solution)/shard_map/dot_general | solution.py:1661
  128.9 0.8 slice_reduce_fusion.3
  129.8 1.5 fusion.21
  131.4 2.1 fusion.23
  133.8 0.8 copy-done
  134.7 1.6 fusion.8
  137.0 1.9 fusion.1
  138.9 1.8 multiply_reduce_fusion.1
  141.5 2.8 multiply_convert_fusion.5
  144.4 3.6 %multiply_reduce_fusion = (f32[512]{0:T(512)S(1)}, bf16[512,1536]{1,0:T(8,128)(2,1)}, bf16[512,1536]{1,0:T(8,128)(2,1)S(1)}) fusion(f32[512,1536]{1,0:T(8,128)S(1)} %copy-done.2, f32[512,3200]{1,0:T(8,128)S(1)} %copy-done.1, bf16[512,768]{1,0:T(8,128)(2,1)S(1)} %get-tuple-element.130, bf16[1536,768]{1,0:T(8,128)(2,1)S(1)} %bitcast.122), kind=kOutput, calls=%fused_computation.6 | convolution fusion | flops 1220541952 | bytes 12584960 | tf_op jit(solution)/shard_map/dot_general | solution.py:1665
  147.9 2.1 pad_maximum_fusion.refs_14_
  150.0 0.9 copy.55.refs_5_
  150.9 4.4 %convolution_convert_fusion = bf16[1536,768]{1,0:T(8,128)(2,1)} fusion(bf16[512,1536]{1,0:T(8,128)(2,1)} %copy-done.6, bf16[512,768]{1,0:T(8,128)(2,1)S(1)} %get-tuple-element.130), kind=kOutput, calls=%fused_computation | convolution fusion | flops 1209139200 | bytes 4718592 | tf_op jit(solution)/shard_map/dot_general | solution.py:1669
  155.3 3.1 %convolution_convert_fusion.1 = bf16[768,1536]{1,0:T(8,128)(2,1)} fusion(bf16[512,1536]{1,0:T(8,128)(2,1)S(1)} %copy-done.23, f32[512,768]{1,0:T(8,128)S(1)} %get-tuple-element.127, f32[768]{0:T(1024)S(1)} %bitcast.111, f32[512]{0:T(512)S(1)} %add_rsqrt_fusion.1, f32[512]{0:T(512)S(1)} %broadcast_multiply_fusion.4), kind=kOutput, calls=%fused_computation.1 | convolution fusion | flops 1210712064 | bytes 5512192 | tf_op jit(solution)/shard_map/dot_general | solution.py:1669
  158.4 3.0 %convolution_convert_fusion.2 = bf16[1536,768]{1,0:T(8,128)(2,1)} fusion(f32[512,768]{1,0:T(8,128)S(1)} %copy-done.5, f32[512,1536]{1,0:T(8,128)S(1)} %copy-done.21), kind=kOutput, calls=%fused_computation.2 | convolution fusion | flops 1213464576 | bytes 7077888 | tf_op jit(solution)/shard_map/dot_general | solution.py:1669
  162.1 118.2 %backward_all.1 = (f32[48,768]{1,0:T(8,128)}, f32[24,1536]{1,0:T(8,128)}, f32[48,768]{1,0:T(8,128)}, f32[24,3200]{1,0:T(8,128)}, f32[24,1536]{1,0:T(8,128)}, /*i...) custom-call(bf16[2,2,4,2,48,768]{5,4,3,2,1,0:T(8,128)(2,1)} %bitcast, ...), custom_call_target="tpu_custom_call" | custom-call | tf_op jit(solution)/shard_map/backward_all/pallas_call | solution.py:1316
  280.3 2.5 convert_element_type.104
  285.6 0.7 slice_reduce_fusion
  287.3 0.9 copy.66
  288.9 0.7 copy.68
  (77 shorter events, 9.8 us)
Async XLA Ops:
  119.8 4.7 %copy-start.1 = (f32[512,3200]{1,0:T(8,128)S(1)}, f32[512,3200]{1,0:T(8,128)}, u32[]{:S(2)}) copy-start(f32[512,3200]{1,0:T(8,128)} %get-tuple-element.49) | copy-start | bytes 19660804
  119.8 4.9 %copy-start.3 = (bf16[4,128,768]{2,1,0:T(8,128)(2,1)S(1)}, bf16[4,128,768]{2,1,0:T(8,128)(2,1)}, u32[]{:S(2)}) copy-start(bf16[4,128,768]{2,1,0:T(8,128)(2,1)} %get-tuple-element.48.refs_3_) | copy-start | bytes 2359300
  123.7 4.9 %copy-start.6 = (bf16[512,1536]{1,0:T(8,128)(2,1)}, bf16[512,1536]{1,0:T(8,128)(2,1)S(1)}, u32[]{:S(2)}) copy-start(bf16[512,1536]{1,0:T(8,128)(2,1)S(1)} %multiply_convert_fusion.3) | copy-start | bytes 4718596
  124.7 5.0 %copy-start.18 = (bf16[2,2,4,2,24,1536]{5,4,3,2,1,0:T(8,128)(2,1)S(1)}, bf16[2,2,4,2,24,1536]{5,4,3,2,1,0:T(8,128)(2,1)}, u32[]{:S(2)}) copy-start(bf16[2,2,4,2,24,1536]{5,4,3,2,1,0:T(8,128)(2,1)} %get-tuple-element.53) | copy-start | bytes 7077892
  129.8 1.7 copy-start.19
  131.3 5.7 %copy-start.20 = (f32[512,1536]{1,0:T(8,128)}, f32[512,1536]{1,0:T(8,128)S(1)}, u32[]{:S(2)}) copy-start(f32[512,1536]{1,0:T(8,128)S(1)} %fusion.21) | copy-start | bytes 9437188
  133.5 1.1 copy-start
  137.0 1.9 copy-start.4
  138.9 1.8 copy-start.22
  141.5 2.8 copy-start.2
  141.5 2.9 copy-start.17
  150.9 4.4 %copy-start.23 = (bf16[512,1536]{1,0:T(8,128)(2,1)S(1)}, bf16[512,1536]{1,0:T(8,128)(2,1)}, u32[]{:S(2)}) copy-start(bf16[512,1536]{1,0:T(8,128)(2,1)} %copy-done.22) | copy-start | bytes 4718596
  155.3 3.1 %copy-start.5 = (f32[512,768]{1,0:T(8,128)S(1)}, f32[512,768]{1,0:T(8,128)}, u32[]{:S(2)}) copy-start(f32[512,768]{1,0:T(8,128)} %copy-done.4) | copy-start | bytes 4718596
  155.3 3.1 %copy-start.21 = (f32[512,1536]{1,0:T(8,128)S(1)}, f32[512,1536]{1,0:T(8,128)}, u32[]{:S(2)}) copy-start(f32[512,1536]{1,0:T(8,128)} %copy-done.20) | copy-start | bytes 9437188
  158.4 3.0 %copy-start.14 = (f32[128]{0:T(128)S(1)}, f32[128]{0:T(128)}, u32[]{:S(2)}) copy-start(f32[128]{0:T(128)} %param.34) | copy-start | bytes 1540
  158.4 3.0 %copy-start.15 = (f32[128]{0:T(128)S(1)}, f32[128]{0:T(128)}, u32[]{:S(2)}) copy-start(f32[128]{0:T(128)} %param.36) | copy-start | bytes 1540
  280.3 2.5 copy-start.9
  280.3 6.0 %copy-start.16 = (f32[8,128]{1,0:T(8,128)S(1)}, f32[8,128]{1,0:T(8,128)}, u32[]{:S(2)}) copy-start(f32[8,128]{1,0:T(8,128)} %get-tuple-element.77) | copy-start | bytes 12292
  280.3 7.1 %copy-start.7 = (bf16[2,2,128,768]{3,2,1,0:T(8,128)(2,1)S(1)}, bf16[2,2,128,768]{3,2,1,0:T(8,128)(2,1)}, u32[]{:S(2)}) copy-start(bf16[2,2,128,768]{3,2,1,0:T(8,128)(2,1)} %get-tuple-element.164) | copy-start | bytes 2359300
  280.3 7.9 %copy-start.13 = (f32[24,1536]{1,0:T(8,128)S(1)}, f32[24,1536]{1,0:T(8,128)}, u32[]{:S(2)}) copy-start(f32[24,1536]{1,0:T(8,128)} %get-tuple-element.166) | copy-start | bytes 442372
  282.8 6.1 %copy-start.8 = (f32[24,3200]{1,0:T(8,128)S(1)}, f32[24,3200]{1,0:T(8,128)}, u32[]{:S(2)}) copy-start(f32[24,3200]{1,0:T(8,128)} %get-tuple-element.167) | copy-start | bytes 921604
  282.8 6.8 %copy-start.12 = (f32[48,768]{1,0:T(8,128)S(1)}, f32[48,768]{1,0:T(8,128)}, u32[]{:S(2)}) copy-start(f32[48,768]{1,0:T(8,128)} %get-tuple-element.168) | copy-start | bytes 442372
  282.8 7.5 %copy-start.11 = (f32[24,1536]{1,0:T(8,128)S(1)}, f32[24,1536]{1,0:T(8,128)}, u32[]{:S(2)}) copy-start(f32[24,1536]{1,0:T(8,128)} %get-tuple-element.169) | copy-start | bytes 442372
  284.9 6.0 %copy-start.10 = (f32[48,768]{1,0:T(8,128)S(1)}, f32[48,768]{1,0:T(8,128)}, u32[]{:S(2)}) copy-start(f32[48,768]{1,0:T(8,128)} %get-tuple-element.170) | copy-start | bytes 442372
